TPU v7x, 128 devices: a whole 4x4x4 slice. The times are simulated.
128 devices in a mesh: img: 32 (over z, y_hi, x), blk: 4 (over y_lo, core).
Axes of the slice: x: 4, y: 4 (y_hi: 2, y_lo: 2; y = y_hi * 2 + y_lo), z: 4, core: 2. Of those that a mesh axis runs over, the one named last changes fastest.
Arguments:
- patches: bfloat16 [1024, 64, 1024], P('blk', 'img'), may hold values from -6 to 6
- cls_tokens: bfloat16 [64, 1024], P('img'), may hold values from -6 to 6
- patch_masks: int32 [1024, 64], P('blk', 'img'), may hold values from 0 to 1, as said below
- mask_token: bfloat16 [1024], replicated, may hold values from -4 to 4
- pos_embed: bfloat16 [1024, 1024], P('blk'), may hold values from -3 to 3
- ln1_gain: float32 [1024], replicated, may hold values from 0.5 to 1.5
- ln1_bias: float32 [1024], replicated, may hold values from -1 to 1
- qkv_weight: bfloat16 [1024, 3072], replicated, may hold values from -0.1875 to 0.1875
- qv_bias: float32 [2048], replicated, may hold values from -3 to 3
- proj_weight: bfloat16 [1024, 1024], replicated, may hold values from -1.5 to 1.5
- proj_bias: float32 [1024], replicated, may hold values from -2 to 2
- scale_attn: float32 [1024], replicated, may hold values from 0.5 to 2
- ln2_gain: float32 [1024], replicated, may hold values from 0.5 to 1.5
- ln2_bias: float32 [1024], replicated, may hold values from -1 to 1
- fc1_weight: bfloat16 [1024, 4096], replicated, may hold values from -0.1875 to 0.1875
- fc1_bias: float32 [4096], replicated, may hold values from -3 to 3
- fc2_weight: bfloat16 [4096, 1024], replicated, may hold values from -0.09375 to 0.09375
- fc2_bias: float32 [1024], replicated, may hold values from -2 to 2
- scale_mlp: float32 [1024], replicated, may hold values from 0.5 to 2
- cot_patches: bfloat16 [1024, 64, 1024], P('blk', 'img'), may hold values from -6 to 6
- cot_cls: bfloat16 [64, 1024], P('img'), may hold values from -6 to 6
Outputs:
- out_patches: bfloat16 [1024, 64, 1024], P('blk', 'img')
- out_cls: bfloat16 [64, 1024], P('img')
- grad_patches: float32 [1024, 64, 1024], P('blk', 'img')
- grad_cls: float32 [64, 1024], P('img')
- grad_mask_token: float32 [1024], P(('img', 'blk'))
- grad_pos_embed: float32 [1024, 1024], P('blk', 'img')
- grad_ln1_gain: float32 [1024], P(('img', 'blk'))
- grad_ln1_bias: float32 [1024], P(('img', 'blk'))
- grad_qkv_weight: float32 [1024, 3072], P(('img', 'blk'))
- grad_qv_bias: float32 [2048], P(('img', 'blk'))
- grad_proj_weight: float32 [1024, 1024], P(('img', 'blk'))
- grad_proj_bias: float32 [1024], P(('img', 'blk'))
- grad_scale_attn: float32 [1024], P(('img', 'blk'))
- grad_ln2_gain: float32 [1024], P(('img', 'blk'))
- grad_ln2_bias: float32 [1024], P(('img', 'blk'))
- grad_fc1_weight: float32 [1024, 4096], P(('img', 'blk'))
- grad_fc1_bias: float32 [4096], P(('img', 'blk'))
- grad_fc2_weight: float32 [4096, 1024], P(('img', 'blk'))
- grad_fc2_bias: float32 [1024], P(('img', 'blk'))
- grad_scale_mlp: float32 [1024], P(('img', 'blk'))
Inputs may be any that keep to these rules, and one draw needn't show every extreme that they name: `patch_masks`: each crop masks between 102 and 512 of its patches (inclusive).
All inputs are finite; a program needn't handle non-finite values.
Results may differ from a plain program's by a relative error of at most 0.012.
Values may be sent and summed in bfloat16 or wider, within the bound.
No kernel may reach another device: no remote copies, remote signals or barrier semaphores. Data moves between devices by JAX's collectives and lax.ppermute only.
A program may use at most 448 MiB of HBM per device.

v0:
```python
import jax
import jax.numpy as jnp
from jax import lax
from jax.sharding import PartitionSpec as P

HEADS = 16
HEAD_DIM = 64
MICRO = 2
CROPS_MB = 1


EPS = 1e-06


def side_by_side(arrays, axis, dim, along):
    ends, at = ([], 0)
    for a in arrays[:-1]:
        at += a.shape[along]
        ends.append(at)
    both = jnp.concatenate(arrays, axis=along)
    return tuple(jnp.split(lax.all_gather(both, axis, axis=dim, tiled=True), ends, axis=along))


def copy_for_each(x, axis):
    copies = jnp.broadcast_to(x, (lax.axis_size(axis), *x.shape))
    return lax.all_to_all(copies, axis, split_axis=0, concat_axis=0, tiled=True)


def of_everyone(x, axis):
    return copy_for_each(x, axis).sum(axis=0)


def packed_total(arrays, axis):
    ravelled, at, outs = (jnp.concatenate([a.reshape(-1) for a in arrays]), 0, [])
    total = of_everyone(ravelled, axis)
    for a in arrays:
        outs.append(total[at : at + a.size].reshape(a.shape))
        at += a.size
    return tuple(outs)


def in_blocks(x, dim, size):
    before, after = (x.shape[:dim], x.shape[dim + 1 :])
    return jnp.moveaxis(x.reshape(*before, size, -1, *after), dim, 0)


def sum_at_owner(x, axis, dim):
    pieces = in_blocks(x, dim, lax.axis_size(axis))
    arrived = lax.all_to_all(pieces, axis, split_axis=0, concat_axis=0, tiled=True)
    return arrived.sum(axis=0)


def sum_packed(arrays, axis, dims):
    size = lax.axis_size(axis)
    pieces = [in_blocks(a, dim, size) for a, dim in zip(arrays, dims)]
    lines = jnp.concatenate([b.reshape(size, -1) for b in pieces], axis=1)
    span = max(16, -(-lines.shape[1] // 1024) * 8)
    lines = jnp.pad(lines, ((0, 0), (0, span * 128 - lines.shape[1]))).reshape(-1, 128)
    ravelled, at, outs = (lax.psum_scatter(lines, axis, tiled=True).reshape(-1), 0, [])
    for b in pieces:
        part = b[0]
        outs.append(ravelled[at : at + part.size].reshape(part.shape))
        at += part.size
    return tuple(outs)


def normalize(values):
    center = values - jnp.mean(values, -1, keepdims=True)
    spread = jnp.mean(center * center, -1, keepdims=True)
    return center * lax.rsqrt(spread + EPS)


def exact_gelu(values):
    return jax.nn.gelu(values, approximate=False)


def dot_rows(left, right):
    return jnp.dot(left, right, preferred_element_type=jnp.float32)


def dot_transposed(left, right):
    return lax.dot_general(
        left, right, (((1,), (1,)), ((), ())), preferred_element_type=jnp.float32
    )


def dot_outer(left, right):
    return lax.dot_general(
        left, right, (((0,), (0,)), ((), ())), preferred_element_type=jnp.float32
    )


def column_sum(values):
    return jnp.sum(values.astype(jnp.float32), 0)


def scores_of(queries_h, key_cls, key_heads):
    cls_part = jnp.einsum("rche,che->chr", queries_h, key_cls, preferred_element_type=jnp.float32)
    patch_part = jnp.einsum(
        "rche,kche->chrk", queries_h, key_heads, preferred_element_type=jnp.float32
    )
    return jnp.concatenate((cls_part[..., None], patch_part), -1) * 0.125


def local(
    patches,
    cls_tokens,
    patch_masks,
    mask_token,
    pos_embed,
    ln1_gain,
    ln1_bias,
    qkv_weight,
    qv_bias,
    proj_weight,
    proj_bias,
    scale_attn,
    ln2_gain,
    ln2_bias,
    fc1_weight,
    fc1_bias,
    fc2_weight,
    fc2_bias,
    scale_mlp,
    cot_patches,
    cot_cls,
):
    patch_dev = patches.shape[0]
    width = patches.shape[2]
    crops_here = CROPS_MB
    rows_all = (patch_dev + 1) * crops_here
    head_shape = (HEADS, HEAD_DIM)
    first_flag = (lax.axis_index("blk") == 0).astype(jnp.float32)
    row_weight = jnp.concatenate(
        (
            jnp.ones((crops_here, 1), jnp.float32) * first_flag,
            jnp.ones((patch_dev * crops_here, 1), jnp.float32),
        ),
        0,
    )
    row_weight_low = row_weight.astype(jnp.bfloat16)
    query_weight = jnp.concatenate(
        (jnp.ones((1,), jnp.float32) * first_flag, jnp.ones((patch_dev,), jnp.float32))
    ).astype(jnp.bfloat16)[:, None]
    mask_float = mask_token.astype(jnp.float32)
    position_rows = pos_embed.astype(jnp.float32)[:, None, :]
    acc_mask = jnp.zeros((width,), jnp.float32)
    acc_position = jnp.zeros((patch_dev, width), jnp.float32)
    acc_ln1_gain = jnp.zeros((width,), jnp.float32)
    acc_ln1_bias = jnp.zeros((width,), jnp.float32)
    acc_qkv = jnp.zeros(qkv_weight.shape, jnp.float32)
    acc_qv_bias = jnp.zeros(qv_bias.shape, jnp.float32)
    acc_proj = jnp.zeros(proj_weight.shape, jnp.float32)
    acc_proj_bias = jnp.zeros((width,), jnp.float32)
    acc_scale_attn = jnp.zeros((width,), jnp.float32)
    acc_ln2_gain = jnp.zeros((width,), jnp.float32)
    acc_ln2_bias = jnp.zeros((width,), jnp.float32)
    acc_fc1 = jnp.zeros(fc1_weight.shape, jnp.float32)
    acc_fc1_bias = jnp.zeros(fc1_bias.shape, jnp.float32)
    acc_fc2 = jnp.zeros(fc2_weight.shape, jnp.float32)
    acc_fc2_bias = jnp.zeros((width,), jnp.float32)
    acc_scale_mlp = jnp.zeros((width,), jnp.float32)
    out_patch_parts = []
    out_cls_parts = []
    grad_patch_parts = []
    grad_cls_parts = []
    for micro_index in range(MICRO):
        lower = micro_index * crops_here
        upper = lower + crops_here
        patch_vals = patches[:, lower:upper].astype(jnp.float32)
        mask_vals = patch_masks[:, lower:upper].astype(jnp.float32)[..., None]
        cls_vals = cls_tokens[lower:upper].astype(jnp.float32)
        mixed_in = mask_vals * mask_float + (1.0 - mask_vals) * patch_vals + position_rows
        tokens = jnp.concatenate((cls_vals[None], mixed_in), 0).reshape(rows_all, width)
        unit_one, unit_one_back = jax.vjp(normalize, tokens)
        normed_one = (unit_one * ln1_gain + ln1_bias).astype(jnp.bfloat16)
        joined = dot_rows(normed_one, qkv_weight)
        queries = (joined[:, :width] + qv_bias[:width]).astype(jnp.bfloat16)
        key_rows = joined[:, width : 2 * width].astype(jnp.bfloat16)
        value_rows = (joined[:, 2 * width :] + qv_bias[width:]).astype(jnp.bfloat16)
        queries_h = queries.reshape((patch_dev + 1, crops_here) + head_shape)
        key_cls = key_rows[:crops_here].reshape((crops_here,) + head_shape)
        value_cls = value_rows[:crops_here].reshape((crops_here,) + head_shape)
        key_own = key_rows[crops_here:].reshape(patch_dev, crops_here, width)
        value_own = value_rows[crops_here:].reshape(patch_dev, crops_here, width)
        key_all, value_all = side_by_side((key_own, value_own), "blk", 0, 1)
        key_heads = key_all.reshape((-1, crops_here) + head_shape)
        value_heads = value_all.reshape((-1, crops_here) + head_shape)
        scores = scores_of(queries_h, key_cls, key_heads)
        top_score = jnp.max(scores, -1, keepdims=True)
        expo = jnp.exp(scores - top_score)
        expo_total = jnp.sum(expo, -1, keepdims=True)
        probs = expo / expo_total
        log_total = top_score + jnp.log(expo_total)
        weights_low = probs.astype(jnp.bfloat16)
        mixed = jnp.einsum(
            "chrk,kche->rche", weights_low[..., 1:], value_heads, preferred_element_type=jnp.float32
        ) + jnp.einsum(
            "chr,che->rche", weights_low[..., 0], value_cls, preferred_element_type=jnp.float32
        )
        attended = mixed.reshape(rows_all, width).astype(jnp.bfloat16)
        branch_one = dot_rows(attended, proj_weight) + proj_bias
        hidden = tokens + scale_attn * branch_one
        unit_two, unit_two_back = jax.vjp(normalize, hidden)
        normed_two = (unit_two * ln2_gain + ln2_bias).astype(jnp.bfloat16)
        pre_act = dot_rows(normed_two, fc1_weight) + fc1_bias
        activ, gelu_back = jax.vjp(exact_gelu, pre_act)
        activ_low = activ.astype(jnp.bfloat16)
        branch_two = dot_rows(activ_low, fc2_weight) + fc2_bias
        output = hidden + scale_mlp * branch_two
        out_rows = output.reshape(patch_dev + 1, crops_here, width).astype(jnp.bfloat16)
        out_cls_parts.append(out_rows[0])
        out_patch_parts.append(out_rows[1:])
        g_out = jnp.concatenate(
            (
                cot_cls[lower:upper].astype(jnp.float32)[None],
                cot_patches[:, lower:upper].astype(jnp.float32) * mask_vals,
            ),
            0,
        )
        g_out = g_out.reshape(rows_all, width)
        acc_scale_mlp = acc_scale_mlp + jnp.sum(g_out * branch_two * row_weight, 0)
        g_branch_two = (scale_mlp * g_out).astype(jnp.bfloat16)
        weighted_two = g_branch_two * row_weight_low
        acc_fc2_bias = acc_fc2_bias + column_sum(weighted_two)
        acc_fc2 = acc_fc2 + dot_outer(activ_low, weighted_two)
        g_activ = dot_transposed(g_branch_two, fc2_weight)
        g_pre = gelu_back(g_activ)[0].astype(jnp.bfloat16)
        weighted_pre = g_pre * row_weight_low
        acc_fc1_bias = acc_fc1_bias + column_sum(weighted_pre)
        acc_fc1 = acc_fc1 + dot_outer(normed_two, weighted_pre)
        g_normed_two = dot_transposed(g_pre, fc1_weight)
        acc_ln2_gain = acc_ln2_gain + jnp.sum(g_normed_two * unit_two * row_weight, 0)
        acc_ln2_bias = acc_ln2_bias + jnp.sum(g_normed_two * row_weight, 0)
        g_hidden = g_out + unit_two_back(g_normed_two * ln2_gain)[0]
        acc_scale_attn = acc_scale_attn + jnp.sum(g_hidden * branch_one * row_weight, 0)
        g_branch_one = (scale_attn * g_hidden).astype(jnp.bfloat16)
        weighted_one = g_branch_one * row_weight_low
        acc_proj_bias = acc_proj_bias + column_sum(weighted_one)
        acc_proj = acc_proj + dot_outer(attended, weighted_one)
        g_attended = dot_transposed(g_branch_one, proj_weight).astype(jnp.bfloat16)
        g_att_h = g_attended.reshape((patch_dev + 1, crops_here) + head_shape)
        scores_back = scores_of(queries_h, key_cls, key_heads)
        probs_back = jnp.exp(scores_back - log_total)
        g_probs = jnp.concatenate(
            (
                jnp.einsum("rche,che->chr", g_att_h, value_cls, preferred_element_type=jnp.float32)[
                    ..., None
                ],
                jnp.einsum(
                    "rche,kche->chrk", g_att_h, value_heads, preferred_element_type=jnp.float32
                ),
            ),
            -1,
        )
        inner = jnp.sum(probs_back * g_probs, -1, keepdims=True)
        g_scores = (probs_back * (g_probs - inner)).astype(jnp.bfloat16)
        g_queries = (
            jnp.einsum(
                "chrk,kche->rche", g_scores[..., 1:], key_heads, preferred_element_type=jnp.float32
            )
            + jnp.einsum(
                "chr,che->rche", g_scores[..., 0], key_cls, preferred_element_type=jnp.float32
            )
        ) * 0.125
        g_queries = g_queries.reshape(rows_all, width).astype(jnp.bfloat16)
        scores_kept = g_scores * query_weight
        weights_kept = probs_back.astype(jnp.bfloat16) * query_weight
        count = lax.axis_size("blk") * patch_dev
        score_part = lax.dynamic_slice_in_dim(scores_kept, 1, count, 3)
        weight_part = lax.dynamic_slice_in_dim(weights_kept, 1, count, 3)
        key_part = (
            jnp.einsum("chrk,rche->kche", score_part, queries_h, preferred_element_type=jnp.float32)
            * 0.125
        )
        value_part = jnp.einsum(
            "chrk,rche->kche", weight_part, g_att_h, preferred_element_type=jnp.float32
        )
        kv_grads = lax.psum_scatter(
            jnp.concatenate(
                (
                    key_part.reshape(count, crops_here, width),
                    value_part.reshape(count, crops_here, width),
                ),
                -1,
            ),
            "blk",
            scatter_dimension=0,
            tiled=True,
        )
        g_key_cls = (
            jnp.einsum(
                "chr,rche->che", scores_kept[..., 0], queries_h, preferred_element_type=jnp.float32
            )
            * 0.125
        )
        g_value_cls = jnp.einsum(
            "chr,rche->che", weights_kept[..., 0], g_att_h, preferred_element_type=jnp.float32
        )
        g_key_cls, g_value_cls = packed_total((g_key_cls, g_value_cls), "blk")
        g_keys = jnp.concatenate(
            (
                g_key_cls.reshape(crops_here, width),
                kv_grads[..., :width].reshape(patch_dev * crops_here, width),
            ),
            0,
        )
        g_values = jnp.concatenate(
            (
                g_value_cls.reshape(crops_here, width),
                kv_grads[..., width:].reshape(patch_dev * crops_here, width),
            ),
            0,
        )
        g_joined = jnp.concatenate(
            (g_queries, g_keys.astype(jnp.bfloat16), g_values.astype(jnp.bfloat16)), -1
        )
        weighted_joined = g_joined * row_weight_low
        acc_qv_bias = acc_qv_bias + jnp.concatenate(
            (column_sum(weighted_joined[:, :width]), column_sum(weighted_joined[:, 2 * width :]))
        )
        acc_qkv = acc_qkv + dot_outer(normed_one, weighted_joined)
        g_normed_one = dot_transposed(g_joined, qkv_weight)
        acc_ln1_gain = acc_ln1_gain + jnp.sum(g_normed_one * unit_one * row_weight, 0)
        acc_ln1_bias = acc_ln1_bias + jnp.sum(g_normed_one * row_weight, 0)
        g_tokens = g_hidden + unit_one_back(g_normed_one * ln1_gain)[0]
        g_rows = g_tokens.reshape(patch_dev + 1, crops_here, width)
        grad_cls_parts.append(g_rows[0])
        grad_patch_parts.append(g_rows[1:] * (1.0 - mask_vals))
        acc_mask = acc_mask + jnp.sum(g_rows[1:] * mask_vals, (0, 1))
        acc_position = acc_position + jnp.sum(g_rows[1:], 1)
    out_patches = jnp.concatenate(out_patch_parts, 1)
    out_cls = jnp.concatenate(out_cls_parts, 0)
    grad_patches = jnp.concatenate(grad_patch_parts, 1)
    grad_cls = jnp.concatenate(grad_cls_parts, 0)
    grad_position = sum_at_owner(acc_position, "img", 1)
    summed = tuple(
        sum_packed(
            (
                acc_mask,
                acc_ln1_gain,
                acc_ln1_bias,
                acc_qkv,
                acc_qv_bias,
                acc_proj,
                acc_proj_bias,
                acc_scale_attn,
                acc_ln2_gain,
                acc_ln2_bias,
                acc_fc1,
                acc_fc1_bias,
                acc_fc2,
                acc_fc2_bias,
                acc_scale_mlp,
            ),
            ("img", "blk"),
            (0, 0, 0, 0, 0, 0, 0, 0, 0, 0, 0, 0, 0, 0, 0),
        )
    )
    return (out_patches, out_cls, grad_patches, grad_cls, summed[0], grad_position) + summed[1:]


def solution(mesh):
    placed = (
        P("blk", "img", None),
        P("img", None),
        P("blk", "img"),
        P(),
        P("blk", None),
        P(),
        P(),
        P(),
        P(),
        P(),
        P(),
        P(),
        P(),
        P(),
        P(),
        P(),
        P(),
        P(),
        P(),
        P("blk", "img", None),
        P("img", None),
    )
    return jax.shard_map(
        local,
        mesh=mesh,
        in_specs=placed,
        out_specs=(
            P("blk", "img", None),
            P("img", None),
            P("blk", "img", None),
            P("img", None),
            P(("img", "blk")),
            P("blk", "img"),
            P(("img", "blk")),
            P(("img", "blk")),
            P(("img", "blk"), None),
            P(("img", "blk")),
            P(("img", "blk"), None),
            P(("img", "blk")),
            P(("img", "blk")),
            P(("img", "blk")),
            P(("img", "blk")),
            P(("img", "blk"), None),
            P(("img", "blk")),
            P(("img", "blk"), None),
            P(("img", "blk")),
            P(("img", "blk")),
        ),
        check_vma=False,
    )
```

profile of v0, /device:TPU:0, one launch (start us, length us, event | category | flops | bytes accessed | tf_op | source)
XLA Modules:
  0.0 1644.1 jit_solution(17811071558544459348)
XLA Ops:
  39.1 3.4 convolution_bitcast_fusion.6
  45.2 29.1 %all-gather.5.cloned.1.call-done = bf16[1024,2,1024]{2,0,1:T(8,128)(2,1)} async-done(((bf16[256,2,1024]{2,0,1:T(8,128)(2,1)}), bf16[1024,2,1024]{2,0,1:T(8,128)(2,1)}) %all-gather.5.cloned.1.call-update) | async-done | bytes 4194320 | tf_op jit(solution)/shard_map/all_gather | solution.py:21
  74.4 4.7 fusion.69
  79.0 4.1 copy.150
  83.1 4.4 convolution_bitcast_fusion.2
  87.6 7.2 fusion.58
  94.8 8.8 fusion.1
  104.2 10.2 divide_convert_fusion
  114.4 9.0 all-gather.3.cloned.1.call-done
  123.5 4.7 fusion.68
  128.1 4.0 copy.145
  132.1 4.4 convolution_bitcast_fusion.3
  136.5 7.4 fusion.59
  144.0 8.8 fusion
  152.8 10.3 divide_convert_fusion.1
  163.7 3.9 copy.148
  169.3 4.3 copy.143
  175.6 8.0 add_convert_fusion.2
  185.5 3.7 add_convert_fusion.3
  192.0 16.4 multiply_convert_fusion.3
  208.4 14.9 multiply_convert_fusion.2
  223.3 13.2 add_convert_fusion.1
  236.5 14.6 convert_reduce_fusion
  251.1 6.6 fusion.81
  257.8 8.2 multiply_reduce_fusion.7
  266.1 5.1 fusion.63
  271.3 5.3 multiply_reduce_fusion.2
  280.6 10.3 convolution_bitcast_fusion
  294.3 10.1 convolution_bitcast_fusion.1
  306.0 19.0 %multiply_reduce_fusion = f32[16,257]{1,0:T(8,128)S(1)} fusion(f32[1,16,257,1024]{3,2,1,0:T(8,128)} %convolution_bitcast_fusion, f32[1,16,257,1]{3,2,1,0:T(8,128)S(1)} %copy-done.14, f32[16,257]{1,0:T(8,128)S(1)} %copy-done.78, f32[1,16,257,1024]{3,2,1,0:T(8,128)} %copy-done.2, f32[1,16,257,1]{3,2,1,0:T(8,128)S(1)} %copy-done.5), kind=kLoop, calls=%fused_computation.5 | loop fusion | flops 25284688 | bytes 33751296 | tf_op jit(solution)/shard_map/reduce_sum | solution.py:256
  325.1 17.6 %multiply_reduce_fusion.1 = f32[16,257]{1,0:T(8,128)S(1)} fusion(f32[1,16,257,1024]{3,2,1,0:T(8,128)} %convolution_bitcast_fusion.1, f32[1,16,257,1]{3,2,1,0:T(8,128)S(1)} %convolution_bitcast_fusion.5, f32[16,257]{1,0:T(8,128)S(1)} %copy-done.79, f32[1,16,257,1024]{3,2,1,0:T(8,128)S(1)} %bitcast.317, f32[1,16,257,1]{3,2,1,0:T(8,128)S(1)} %copy-done.7), kind=kLoop, calls=%fused_computation.8 | loop fusion | flops 25284688 | bytes 33751296 | tf_op jit(solution)/shard_map/reduce_sum | solution.py:256
  342.7 50.0 %broadcast_multiply_fusion = (bf16[1,16,257,1025]{3,2,1,0:T(8,128)(2,1)}, bf16[1,16,257,1025]{3,2,1,0:T(8,128)(2,1)}, bf16[1,16,257,1025]{3,2,1,0:T(8,128)(2,1)}...) fusion(bf16[257]{0:T(512)(128)(2,1)S(1)} %copy-done.148, ...), kind=kLoop, calls=%fused_computation.49 | loop fusion | flops 84296000 | bytes 118080704 | tf_op jit(solution)/shard_map/mul | solution.py:267
  392.8 6.8 fusion.6
  402.7 4.1 pad_maximum_fusion.3
  407.3 6.7 fusion.9
  414.1 7.4 broadcast_multiply_fusion.3
  421.6 4.2 pad_maximum_fusion.2
  432.8 4.0 all-to-all-start.1
  449.7 4.7 fusion.36
  454.4 8.9 fusion.27
  463.4 8.4 multiply_convert_fusion.4
  471.8 8.2 multiply_convert_fusion.5
  480.0 13.0 convolution_add_fusion
  493.0 12.9 convolution_add_fusion.1
  506.0 5.0 reshape_reshape.33
  513.3 18.3 %reshape_reshape.34 = f32[128,32768]{1,0:T(8,128)} reshape(f32[1024,4096]{1,0:T(8,128)} %convolution_add_fusion.1) | data formatting | bytes 33554432 | tf_op jit(solution)/shard_map/reshape;reshape | solution.py:56
  531.7 18.4 %reshape_reshape.35 = f32[128,32768]{1,0:T(8,128)} reshape(f32[4096,1024]{1,0:T(8,128)} %convolution_add_fusion) | data formatting | bytes 33554432 | tf_op jit(solution)/shard_map/reshape;reshape | solution.py:56
  552.1 3.8 all-to-all-start
  563.9 6.6 reduce-scatter.7.cloned.1.call-done
  572.5 6.0 fusion.51
  578.7 10.9 broadcast_multiply_fusion.4
  589.7 4.2 multiply_reduce_fusion.13
  600.1 5.6 fusion.55
  606.4 7.2 convolution_add_fusion.2
  613.6 12.2 reshape_reshape.32
  631.6 45.2 %dynamic-update-slice.3 = f32[128,98424]{1,0:T(8,128)} dynamic-update-slice(f32[128,98424]{1,0:T(8,128)} %dynamic-update-slice.2, f32[128,24576]{1,0:T(8,128)} %reshape_reshape.32, s32[]{} %constant.136, s32[]{} %constant.139) | dynamic-update-slice | bytes 25165828
  678.5 23.1 %dynamic-update-slice.5 = f32[128,98424]{1,0:T(8,128)} dynamic-update-slice(f32[128,98424]{1,0:T(8,128)} %dynamic-update-slice.4, f32[128,8192]{1,0:T(8,128)} %reshape_reshape.33, s32[]{} %constant.136, s32[]{} %constant.141) | dynamic-update-slice | bytes 8388612
  708.5 55.9 %dynamic-update-slice.10 = f32[128,98424]{1,0:T(8,128)} dynamic-update-slice(f32[128,98424]{1,0:T(8,128)} %dynamic-update-slice.9, f32[128,32768]{1,0:T(8,128)} %reshape_reshape.34, s32[]{} %constant.136, s32[]{} %constant.146) | dynamic-update-slice | bytes 33554436
  766.1 54.8 %dynamic-update-slice.12 = f32[128,98424]{1,0:T(8,128)} dynamic-update-slice(f32[128,98424]{1,0:T(8,128)} %dynamic-update-slice.11, f32[128,32768]{1,0:T(8,128)} %reshape_reshape.35, s32[]{} %constant.136, s32[]{} %constant.148) | dynamic-update-slice | bytes 33554436
  824.0 33.8 %pad.7 = f32[128,99328]{1,0:T(8,128)} pad(f32[128,98424]{1,0:T(8,128)} %dynamic-update-slice.14, f32[]{:T(128)} %constant.40.clone.1), padding=0_0x0_904 | pad | bytes 101249024 | tf_op jit(solution)/shard_map/jit(_pad)/pad | solution.py:58
  857.8 38.1 %reshape.1233 = f32[99328,128]{1,0:T(8,128)} reshape(f32[128,99328]{1,0:T(8,128)} %pad.7) | data formatting | bytes 101711872 | tf_op jit(solution)/shard_map/reshape | solution.py:58
  898.4 9.5 all-to-all-start.2
  918.3 11.0 all-to-all-done.2
  931.2 696.6 %reduce-scatter.11.cloned.1.call-done = f32[776,128]{1,0:T(8,128)} async-done(((f32[99328,128]{1,0:T(8,128)}), f32[776,128]{1,0:T(8,128)}) %reduce-scatter.11.cloned.1.call-update) | async-done | bytes 397328
  (544 shorter events, 140.2 us)
Async XLA Ops:
  7.2 176.4 %copy-start = (bf16[1024,1024]{1,0:T(8,128)(2,1)S(1)}, bf16[1024,1024]{1,0:T(8,128)(2,1)}, u32[]{:S(2)}) copy-start(bf16[1024,1024]{1,0:T(8,128)(2,1)} %param.30) | copy-start | bytes 6291460
  7.2 67.1 %all-gather.5.cloned.1.call-start = ((), (), s32[]{:S(2)}) async-start(), calls=%async_computation.7 | async-start | bytes 5242880 | tf_op jit(solution)/shard_map/all_gather | solution.py:21
  12.3 176.9 %copy-start.81 = (f32[1,1,1024]{2,0,1:T(1,128)}, f32[1,1,1024]{2,0,1:T(1,128)S(1)}, u32[]{:S(2)}) copy-start(f32[1,1,1024]{2,0,1:T(1,128)S(1)} %get-tuple-element.236) | copy-start | bytes 12292
  12.3 176.9 %copy-start.83 = (f32[1,1,1024]{2,0,1:T(1,128)}, f32[1,1,1024]{2,0,1:T(1,128)S(1)}, u32[]{:S(2)}) copy-start(f32[1,1,1024]{2,0,1:T(1,128)S(1)} %get-tuple-element.235) | copy-start | bytes 12292
  14.4 174.8 %copy-start.9 = (f32[256,1,1024]{2,0,1:T(8,128)}, f32[256,1,1024]{2,0,1:T(8,128)S(1)}, u32[]{:S(2)}) copy-start(f32[256,1,1024]{2,0,1:T(8,128)S(1)} %get-tuple-element.207) | copy-start | bytes 3145732
  25.7 97.7 %all-gather.3.cloned.1.call-start = ((), (), s32[]{:S(2)}) async-start(), calls=%async_computation.6 | async-start | bytes 5242880 | tf_op jit(solution)/shard_map/all_gather | solution.py:21
  27.0 12.1 copy-start.124
  29.3 532.8 %reduce-scatter.9.cloned.1.call-start = ((), (), s32[]{:S(2)}) async-start(), calls=%async_computation.9 | async-start | bytes 10485760 | tf_op jit(solution)/shard_map/reduce_scatter | solution.py:279
  30.1 14.6 copy-start.113
  31.6 13.1 copy-start.115
  32.9 460.1 %copy-start.91 = (bf16[257]{0:T(512)(128)(2,1)}, bf16[257]{0:T(512)(128)(2,1)S(1)}, u32[]{:S(2)}) copy-start(bf16[257]{0:T(512)(128)(2,1)S(1)} %convert_reduce_fusion.14) | copy-start | bytes 1546
  39.1 410.5 %copy-start.93 = (f32[1,1,1024]{2,0,1:T(1,128)}, f32[1,1,1024]{2,0,1:T(1,128)S(1)}, u32[]{:S(2)}) copy-start(f32[1,1,1024]{2,0,1:T(1,128)S(1)} %get-tuple-element.232) | copy-start | bytes 12292
  39.1 440.9 %copy-start.95 = (f32[1,1,1024]{2,0,1:T(1,128)}, f32[1,1,1024]{2,0,1:T(1,128)S(1)}, u32[]{:S(2)}) copy-start(f32[1,1,1024]{2,0,1:T(1,128)S(1)} %get-tuple-element.231) | copy-start | bytes 12292
  87.6 16.7 %copy-start.2 = (f32[1,16,257,1024]{3,2,1,0:T(8,128)}, f32[1,16,257,1024]{3,2,1,0:T(8,128)S(1)}, u32[]{:S(2)}) copy-start(f32[1,16,257,1024]{3,2,1,0:T(8,128)S(1)} %convolution_bitcast_fusion.2) | copy-start | bytes 50528260
  136.5 16.2 copy-start.3
  189.3 19.1 %slice-start.8 = ((s8[8388608]{0:T(1024)(128)(4,1)}), s8[4194304]{0:T(1024)(128)(4,1)S(1)}, s32[]{:S(2)}) async-start(s8[8388608]{0:T(1024)(128)(4,1)} %bitcast.372), calls=%async_computation.19 | async-start | bytes 8388608
  191.3 74.7 %copy-start.18 = (f32[257,1024]{1,0:T(8,128)}, f32[257,1024]{1,0:T(8,128)S(1)}, u32[]{:S(2)}) copy-start(f32[257,1024]{1,0:T(8,128)S(1)} %get-tuple-element.234) | copy-start | bytes 3158020
  191.3 80.0 %copy-start.25 = (f32[257,1024]{1,0:T(8,128)}, f32[257,1024]{1,0:T(8,128)S(1)}, u32[]{:S(2)}) copy-start(f32[257,1024]{1,0:T(8,128)S(1)} %get-tuple-element.169) | copy-start | bytes 3158020
  191.6 74.4 %copy-start.100 = (f32[257]{0:T(512)}, f32[257]{0:T(512)S(1)}, u32[]{:S(2)}) copy-start(f32[257]{0:T(512)S(1)} %broadcast_multiply_fusion.8) | copy-start | bytes 3088
  191.9 74.1 %copy-start.107 = (f32[257]{0:T(512)}, f32[257]{0:T(512)S(1)}, u32[]{:S(2)}) copy-start(f32[257]{0:T(512)S(1)} %fusion.50) | copy-start | bytes 3088
  192.0 16.4 slice-start.9
  208.3 14.9 copy-start.27
  208.4 14.9 copy-start.125
  223.3 42.8 %copy-start.35 = (bf16[257,4096]{1,0:T(8,128)(2,1)}, bf16[257,4096]{1,0:T(8,128)(2,1)S(1)}, u32[]{:S(2)}) copy-start(bf16[257,4096]{1,0:T(8,128)(2,1)S(1)} %get-tuple-element.170) | copy-start | bytes 6316036
  223.3 13.2 copy-start.30
  251.1 14.9 slice-start.10
  276.7 16.4 copy-start.63
  294.2 30.8 %slice-start = ((s8[17301504]{0:T(1024)(128)(4,1)}), s8[4194304]{0:T(1024)(128)(4,1)S(1)}, s32[]{:S(2)}) async-start(s8[17301504]{0:T(1024)(128)(4,1)} %bitcast.316), calls=%async_computation.11 | async-start | bytes 8388608
  294.3 30.8 %slice-start.1 = ((s8[17301504]{0:T(1024)(128)(4,1)}), s8[4194304]{0:T(1024)(128)(4,1)S(1)}, s32[]{:S(2)}) async-start(s8[17301504]{0:T(1024)(128)(4,1)} %bitcast.316), calls=%async_computation.12 | async-start | bytes 8388608
  306.0 19.0 %copy-start.15 = (f32[1,16,257,1]{3,2,1,0:T(8,128)}, f32[1,16,257,1]{3,2,1,0:T(8,128)S(1)}, u32[]{:S(2)}) copy-start(f32[1,16,257,1]{3,2,1,0:T(8,128)S(1)} %convolution_bitcast_fusion.5) | copy-start | bytes 49348
  306.0 19.1 %slice-start.2 = ((s8[17301504]{0:T(1024)(128)(4,1)}), s8[4194304]{0:T(1024)(128)(4,1)S(1)}, s32[]{:S(2)}) async-start(s8[17301504]{0:T(1024)(128)(4,1)} %bitcast.316), calls=%async_computation.13 | async-start | bytes 8388608
  306.0 19.1 %slice-start.3 = ((s8[17301504]{0:T(1024)(128)(4,1)}), s8[4194304]{0:T(1024)(128)(4,1)S(1)}, s32[]{:S(2)}) async-start(s8[17301504]{0:T(1024)(128)(4,1)} %bitcast.316), calls=%async_computation.14 | async-start | bytes 8388608
  306.0 19.1 %slice-start.4 = ((s8[17301504]{0:T(1024)(128)(4,1)}), s8[524288]{0:T(1024)(128)(4,1)S(1)}, s32[]{:S(2)}) async-start(s8[17301504]{0:T(1024)(128)(4,1)} %bitcast.316), calls=%async_computation.15 | async-start | bytes 1048576
  306.0 19.1 %copy-start.7 = (f32[1,16,257,1]{3,2,1,0:T(8,128)S(1)}, f32[1,16,257,1]{3,2,1,0:T(8,128)}, u32[]{:S(2)}) copy-start(f32[1,16,257,1]{3,2,1,0:T(8,128)} %convolution_bitcast_fusion.7) | copy-start | bytes 49348
  306.0 19.1 %copy-start.79 = (f32[16,257]{1,0:T(8,128)S(1)}, f32[16,257]{1,0:T(8,128)}, u32[]{:S(2)}) copy-start(f32[16,257]{1,0:T(8,128)} %log_add_fusion.1) | copy-start | bytes 49348
  325.1 17.6 %copy-start.148 = (bf16[257]{0:T(512)(128)(2,1)S(1)}, bf16[257]{0:T(512)(128)(2,1)}, u32[]{:S(2)}) copy-start(bf16[257]{0:T(512)(128)(2,1)} %concatenate.239) | copy-start | bytes 1546
  342.7 50.0 %copy-start.24 = (bf16[257,1024]{0,1:T(8,128)(2,1)S(1)}, bf16[257,1024]{0,1:T(8,128)(2,1)}, u32[]{:S(2)}) copy-start(bf16[257,1024]{0,1:T(8,128)(2,1)} %copy-done.23) | copy-start | bytes 1579012
  406.8 163.7 %reduce-scatter.7.cloned.1.call-start = ((), (), s32[]{:S(2)}) async-start(), calls=%async_computation.8 | async-start | bytes 10485760 | tf_op jit(solution)/shard_map/reduce_scatter | solution.py:279
  432.1 12.8 copy-start.44
  432.1 12.8 copy-start.64
  432.8 118.6 %all-to-all-start.1 = ((f32[4,1,2048]{2,1,0:T(1,128)}), f32[4,1,2048]{2,1,0:T(1,128)}, u32[]{:S(2)}, u32[]{:S(2)}) async-start(f32[4,1,2048]{2,1,0:T(1,128)} %broadcast_in_dim.62), calls=%async_computation.2 | async-start | bytes 65536 | tf_op jit(solution)/shard_map/all_to_all | solution.py:26
  480.0 13.0 copy-start.19
  480.0 13.0 copy-start.101
  480.0 13.0 copy-start.108
  513.3 18.3 %copy-start.121 = (f32[4096]{0:T(1024)S(1)}, f32[4096]{0:T(1024)}, u32[]{:S(2)}) copy-start(f32[4096]{0:T(1024)} %get-tuple-element.150) | copy-start | bytes 49156
  513.3 18.3 %copy-start.122 = (f32[4096]{0:T(1024)S(1)}, f32[4096]{0:T(1024)}, u32[]{:S(2)}) copy-start(f32[4096]{0:T(1024)} %get-tuple-element.151) | copy-start | bytes 49156
  531.6 18.4 %copy-start.142 = (f32[1024]{0:T(1024)S(1)}, f32[1024]{0:T(1024)}, u32[]{:S(2)}) copy-start(f32[1024]{0:T(1024)} %get-tuple-element.140) | copy-start | bytes 12292
  531.6 18.4 %copy-start.143 = (f32[1024]{0:T(1024)S(1)}, f32[1024]{0:T(1024)}, u32[]{:S(2)}) copy-start(f32[1024]{0:T(1024)} %get-tuple-element.188) | copy-start | bytes 12292
  531.7 19.1 %copy-start.140 = (f32[1024]{0:T(1024)S(1)}, f32[1024]{0:T(1024)}, u32[]{:S(2)}) copy-start(f32[1024]{0:T(1024)} %get-tuple-element.136) | copy-start | bytes 12292
  531.7 19.1 %copy-start.141 = (f32[1024]{0:T(1024)S(1)}, f32[1024]{0:T(1024)}, u32[]{:S(2)}) copy-start(f32[1024]{0:T(1024)} %get-tuple-element.190) | copy-start | bytes 12292
  552.1 8.1 all-to-all-start
  555.9 1071.9 %reduce-scatter.11.cloned.1.call-start = ((), (), s32[]{:S(2)}) async-start(), calls=%async_computation.10 | async-start | bytes 51253248
  557.1 15.3 copy-start.55
  570.5 19.1 %slice-start.14 = ((s8[6291456]{0:T(1024)(128)(4,1)}), s8[4194304]{0:T(1024)(128)(4,1)S(1)}, s32[]{:S(2)}) async-start(s8[6291456]{0:T(1024)(128)(4,1)} %bitcast.378), calls=%async_computation.25 | async-start | bytes 8388608
  572.5 17.1 %slice-start.15 = ((s8[6291456]{0:T(1024)(128)(4,1)}), s8[2097152]{0:T(1024)(128)(4,1)S(1)}, s32[]{:S(2)}) async-start(s8[6291456]{0:T(1024)(128)(4,1)} %bitcast.378), calls=%async_computation.26 | async-start | bytes 4194304
  578.6 11.0 copy-start.10
  578.6 11.0 copy-start.13
  678.5 24.8 %copy-start.71 = (f32[128,8]{1,0:T(8,128)S(1)}, f32[128,8]{1,0:T(8,128)}, u32[]{:S(2)}) copy-start(f32[128,8]{1,0:T(8,128)} %add.370) | copy-start | bytes 12292
  678.5 26.5 %copy-start.72 = (f32[128,8]{1,0:T(8,128)S(1)}, f32[128,8]{1,0:T(8,128)}, u32[]{:S(2)}) copy-start(f32[128,8]{1,0:T(8,128)} %add.372) | copy-start | bytes 12292
  678.5 28.2 %copy-start.75 = (f32[128,8]{1,0:T(8,128)S(1)}, f32[128,8]{1,0:T(8,128)}, u32[]{:S(2)}) copy-start(f32[128,8]{1,0:T(8,128)} %add.374) | copy-start | bytes 12292
  766.1 54.8 %copy-start.73 = (f32[128,8]{1,0:T(8,128)S(1)}, f32[128,8]{1,0:T(8,128)}, u32[]{:S(2)}) copy-start(f32[128,8]{1,0:T(8,128)} %add.380) | copy-start | bytes 12292
  766.1 56.4 %copy-start.74 = (f32[128,8]{1,0:T(8,128)S(1)}, f32[128,8]{1,0:T(8,128)}, u32[]{:S(2)}) copy-start(f32[128,8]{1,0:T(8,128)} %add.382) | copy-start | bytes 12292
  898.4 30.8 %all-to-all-start.2 = ((f32[32,256,32]{1,2,0:T(8,128)}), f32[32,256,32]{1,2,0:T(8,128)}, u32[]{:S(2)}, u32[]{:S(2)}) async-start(f32[32,256,32]{1,2,0:T(8,128)} %bitcast.92), calls=%async_computation.4 | async-start | bytes 2097152 | tf_op jit(solution)/shard_map/all_to_all | solution.py:49
  914.6 722.8 %copy-start.1 = (bf16[1024,1024]{1,0:T(8,128)(2,1)S(1)}, bf16[1024,1024]{1,0:T(8,128)(2,1)}, u32[]{:S(2)}) copy-start(bf16[1024,1024]{1,0:T(8,128)(2,1)} %param.30) | copy-start | bytes 6291460
  (115 other events, 576.6 us)
Sparse Core Ops, SparseCore 0:
  25.9 48.4 all-gather.4
  76.0 47.3 all-gather.2
  406.9 80.7 reduce-scatter.8
  490.1 80.3 reduce-scatter.6
  896.0 731.7 reduce-scatter.10
where the time goes:
time: 1660 us; the launch traced here: 1640 us
  waiting for transfers between devices  756 us (46%)
  local copies, waits for them, and re-layouts  413 us (25%)
  matrix products  255 us (15%)
  other arithmetic  186 us (11%)
  starting transfers between devices  18 us (1%)
  between operations  16.6 us (1%)
    unnamed x6, waiting for transfers between devices  697 us
    unnamed x358, local copies, waits for them, and re-layouts  210 us
    dot_general x8, matrix products, dot_outer(): lax.dot_general(left, right, (((0,), (0,)), ((), ())), preferred_element_...  56.9 us
    dot_general x8, matrix products, dot_transposed(): lax.dot_general(left, right, (((1,), (1,)), ((), ())), preferred_element_...  55.4 us
    another operation x4, local copies, waits for them, and re-layouts, sum_packed(): lines = jnp.concatenate([b.reshape(size, -1) for b in pieces], axis=1)  53.9 us
    mul x1, other arithmetic, local(): scores_kept = g_scores * query_weight  50 us
    dot_general x8, matrix products, dot_rows(): return jnp.dot(left, right, preferred_element_type=jnp.float32)  49.7 us
    all_gather x2, waiting for transfers between devices, side_by_side(): lax.all_gather(both, axis, axis=dim, tiled=True)  38.2 us
  transfers between devices with their start and end apart: 8, of which 6 were waited for; matrix products, arithmetic and copies ran while one was open for 13% of the time, Pallas kernels for 0%

commit v1 on v0

v1 whole, which is shorter than its diff:
```python
import functools
import itertools

import jax
import jax.numpy as jnp
from jax import lax
from jax.experimental import pallas as pl
from jax.experimental.pallas import tpu as pltpu
from jax.sharding import Mesh
from jax.sharding import PartitionSpec as P

EPS = 1e-06
BF = jnp.bfloat16
F32 = jnp.float32
TAIL = 16
INV_SQRT2 = 0.7071067811865476
INV_SQRT2PI = 0.3989422804014327
PAN = 128

ALL = ("z", "yh", "x", "yl", "core")
SIZES = {"z": 4, "yh": 2, "x": 4, "yl": 2, "core": 2}
Y = ("yh", "yl")


def nn(a, b):
    return jnp.dot(a, b, preferred_element_type=F32)


def nt(a, b):
    return lax.dot_general(a, b, (((1,), (1,)), ((), ())), preferred_element_type=F32)


def tn(a, b):
    return lax.dot_general(a, b, (((0,), (0,)), ((), ())), preferred_element_type=F32)


def params(mib):
    return pltpu.CompilerParams(vmem_limit_bytes=mib << 20)


def cost(macs, nbytes, exps=0):
    return pl.CostEstimate(flops=2 * macs, bytes_accessed=nbytes, transcendentals=exps)


def whole(shape):
    return pl.BlockSpec(shape, lambda *_: (0,) * len(shape))


def sd(shape, dtype=BF):
    return jax.ShapeDtypeStruct(shape, dtype)


def unit_of(x):
    center = x - jnp.mean(x, -1, keepdims=True)
    inv = lax.rsqrt(jnp.mean(center * center, -1, keepdims=True) + EPS)
    return center * inv, inv


def unit_grad(gu, unit, inv):
    return (gu - jnp.mean(gu, -1, keepdims=True) - unit * jnp.mean(gu * unit, -1, keepdims=True)) * inv


def norm_project_body(x_ref, gain_ref, bias_ref, w_ref, add_ref, normed_ref, out_ref):
    @pl.when(pl.program_id(0) == 0)
    def _():
        unit, _ = unit_of(x_ref[...])
        normed_ref[...] = (unit * gain_ref[...] + bias_ref[...]).astype(BF)

    out_ref[...] = (nn(normed_ref[...], w_ref[...]) + add_ref[...]).astype(BF)


def project_body(scale, x_ref, w_ref, add_ref, out_ref):
    out_ref[...] = ((nn(x_ref[...], w_ref[...]) + add_ref[...]) * scale).astype(BF)


def project_call(x, w, add, first, stride, norm=None, scale=1.0, tile=512):
    rows, width = x.shape
    at = lambda i: (0, first + stride * i)
    mat, vec = whole((rows, width)), whole((1, width))
    out = pl.BlockSpec((rows, tile), lambda i: (0, i))
    shape = sd((rows, 2 * tile))
    ins = [pl.BlockSpec((width, tile), at), pl.BlockSpec((1, tile), at)]
    common = dict(grid=(2,), compiler_params=params(32),
                  cost_estimate=cost(rows * width * 2 * tile, 4 * (width * tile + rows * tile)))
    if norm is None:
        return pl.pallas_call(functools.partial(project_body, scale), in_specs=[mat] + ins, out_specs=out,
                              out_shape=shape, name="project", **common)(x, w, add)
    return pl.pallas_call(norm_project_body, in_specs=[mat, vec, vec] + ins, out_specs=[mat, out],
                          out_shape=[sd((rows, width)), shape], name="norm_project", **common)(x, *norm, w, add)


def half_mask(h):
    return (lax.broadcasted_iota(jnp.int32, (1, PAN), 1) // 64) == h


def att_fwd_body(np_, q_ref, ko_ref, vo_ref, kp_ref, vp_ref, *refs, chunk):
    out_ref, lse_ref = refs[-2:]
    rows = q_ref.shape[0]
    k_tail = ko_ref[np_:np_ + TAIL, :]
    v_cls = vo_ref[np_:np_ + 1, :].astype(F32)
    ko, kp = ko_ref[0:np_, :], kp_ref[0:np_, :]
    vo, vp = vo_ref[0:np_, :], vp_ref[0:np_, :]
    for r0 in range(0, rows, chunk):
        q = q_ref[r0:r0 + chunk, :]
        outs, lses = [], []
        for h in range(2):
            qh = jnp.where(half_mask(h), q, jnp.zeros_like(q))
            s1, s2 = nt(qh, ko), nt(qh, kp)
            sc = nt(qh, k_tail)[:, 0:1]
            top = jnp.maximum(jnp.maximum(jnp.max(s1, -1, keepdims=True), jnp.max(s2, -1, keepdims=True)), sc)
            p1, p2, pc = jnp.exp(s1 - top), jnp.exp(s2 - top), jnp.exp(sc - top)
            total = jnp.sum(p1, -1, keepdims=True) + jnp.sum(p2, -1, keepdims=True) + pc
            o = nn(p1.astype(BF), vo) + nn(p2.astype(BF), vp) + pc * v_cls
            outs.append(o / total)
            lses.append(top + jnp.log(total))
        out_ref[r0:r0 + chunk, :] = jnp.where(half_mask(0), outs[0], outs[1]).astype(BF)
        lse_ref[r0:r0 + chunk, :] = jnp.where(half_mask(0), lses[0], lses[1])


def att_fwd_call(q, kv, kv_p, group, pairs, into=None, chunk=264):
    rows, width = q.shape
    np_ = rows - TAIL
    col = lambda a: pl.BlockSpec((rows, PAN), lambda i: (0, a + i))
    at = group * pairs
    ins = [col(at), col(0), col(pairs), col(0), col(pairs)]
    args = [q, kv, kv, kv_p, kv_p]
    if into is not None:
        ins.append(pl.BlockSpec(memory_space=pl.ANY))
        args.append(into)
    return pl.pallas_call(
        functools.partial(att_fwd_body, np_, chunk=chunk),
        grid=(pairs,),
        in_specs=ins,
        out_specs=[col(at), col(0)],
        out_shape=[sd((rows, width)), sd((rows, pairs * PAN), F32)],
        input_output_aliases={} if into is None else {5: 0},
        compiler_params=params(40),
        cost_estimate=cost(rows * 2 * np_ * PAN * 2 * pairs * 2, 2 * rows * PAN * pairs * 8, rows * 2 * np_ * 2 * pairs),
        name="att_fwd",
    )(*args)


def att_bwd_body(np_, q_ref, ko_ref, vo_ref, kp_ref, vp_ref, go_ref, o_ref, lse_ref, dq_ref, own_ref, part_ref):
    q, go = q_ref[...], go_ref[...]
    ko, kp = ko_ref[0:np_, :], kp_ref[0:np_, :]
    vo, vp = vo_ref[0:np_, :], vp_ref[0:np_, :]
    k_tail, v_tail = ko_ref[np_:np_ + TAIL, :], vo_ref[np_:np_ + TAIL, :]
    k_cls = k_tail[0:1].astype(F32)
    qt, gt = q.T, go.T
    qf, gf = q.astype(F32), go.astype(F32)
    prod = gf * o_ref[...].astype(F32)
    dq = dkc = dvc = None
    dk1, dk2, dv1, dv2 = [], [], [], []
    for h in range(2):
        mask = half_mask(h)
        qh = jnp.where(mask, q, jnp.zeros_like(q))
        gh = jnp.where(mask, go, jnp.zeros_like(go))
        delta = jnp.sum(jnp.where(mask, prod, 0.0), -1, keepdims=True)
        lse = lse_ref[:, 64 * h:64 * h + 1]
        qth, gth = qt[64 * h:64 * h + 64], gt[64 * h:64 * h + 64]
        dqh = None
        for k, v, dk, dv in ((ko, vo, dk1, dv1), (kp, vp, dk2, dv2)):
            p = jnp.exp(nt(qh, k) - lse)
            ds = (p * (nt(gh, v) - delta)).astype(BF)
            part = nn(ds, k)
            dqh = part if dqh is None else dqh + part
            dk.append(nn(qth, ds))
            dv.append(nn(gth, p.astype(BF)))
        pc = jnp.exp(nt(qh, k_tail)[:, 0:1] - lse)
        dsc = pc * (nt(gh, v_tail)[:, 0:1] - delta)
        dqh = (dqh + dsc * k_cls) * 0.125
        kc = jnp.sum(dsc * qf, 0, keepdims=True)
        vc = jnp.sum(pc * gf, 0, keepdims=True)
        dq = dqh if h == 0 else jnp.where(mask, dqh, dq)
        dkc = kc if h == 0 else jnp.where(mask, kc, dkc)
        dvc = vc if h == 0 else jnp.where(mask, vc, dvc)
    dq_ref[...] = dq.astype(BF)
    both = lambda parts: jnp.concatenate(parts, 0).T.astype(BF)
    own_ref[0:np_, 0:PAN] = both(dk1)
    own_ref[0:np_, PAN:2 * PAN] = both(dv1)
    part_ref[:, 0:PAN] = both(dk2)
    part_ref[:, PAN:2 * PAN] = both(dv2)
    first = lax.broadcasted_iota(jnp.int32, (TAIL, PAN), 0) == 0
    own_ref[np_:np_ + TAIL, 0:PAN] = jnp.where(first, dkc, 0.0).astype(BF)
    own_ref[np_:np_ + TAIL, PAN:2 * PAN] = jnp.where(first, dvc, 0.0).astype(BF)


def att_bwd_call(q, kv, kv_p, go, o, lse, group, pairs):
    rows = q.shape[0]
    np_ = rows - TAIL
    at = group * pairs
    col = lambda a: pl.BlockSpec((rows, PAN), lambda i: (0, a + i))
    two = lambda n: pl.BlockSpec((n, 2 * PAN), lambda i: (0, i))
    return pl.pallas_call(
        functools.partial(att_bwd_body, np_),
        grid=(pairs,),
        in_specs=[col(at), col(0), col(pairs), col(0), col(pairs), col(at), col(at), col(0)],
        out_specs=[col(0), two(rows), two(np_)],
        out_shape=[sd((rows, pairs * PAN)), sd((rows, pairs * 2 * PAN)), sd((np_, pairs * 2 * PAN))],
        compiler_params=params(48),
        cost_estimate=cost(rows * 2 * np_ * PAN * 5 * pairs * 2, 2 * rows * PAN * pairs * 16, rows * 2 * np_ * 2 * pairs),
        name="att_bwd",
    )(q, kv, kv, kv_p, kv_p, go, o, lse)


def trip_body(np_, pairs, order_ref, dq_ref, own_ref, came_ref, mine_ref, send_ref):
    core = order_ref[0]
    n = pairs // 2 * PAN
    for out_ref, side in ((mine_ref, core), (send_ref, 1 - core)):
        out_ref[:, 0:n] = dq_ref[:, pl.ds(pl.multiple_of(side * n, PAN), n)]
        for j in range(pairs // 2):
            for kind in range(2):
                src = pl.ds(pl.multiple_of(side * 2 * n + (2 * j + kind) * PAN, PAN), PAN)
                dst = slice((1 + kind) * n + j * PAN, (1 + kind) * n + (j + 1) * PAN)
                out_ref[0:np_, dst] = (own_ref[0:np_, src].astype(F32) + came_ref[:, src].astype(F32)).astype(BF)
                out_ref[np_:, dst] = own_ref[np_:, src]


def trip_call(order, dq, own, came):
    rows, n = dq.shape
    np_ = rows - TAIL
    shape = sd((rows, n // 2 * 3))
    return pl.pallas_call(
        functools.partial(trip_body, np_, n // PAN),
        grid_spec=pltpu.PrefetchScalarGridSpec(
            num_scalar_prefetch=1, grid=(1,),
            in_specs=[whole(a.shape) for a in (dq, own, came)],
            out_specs=[whole(shape.shape)] * 2),
        out_shape=[shape, shape],
        compiler_params=params(24),
        cost_estimate=cost(0, 2 * rows * n * 8),
        name="trip",
    )(order, dq, own, came)


def mlp_fwd_body(order_ref, att_ref, tok_ref, wp_ref, bp_ref, sa_ref, gain_ref, bias_ref, w1_ref, b1_ref, w2_ref, b2_ref,
                 sm_ref, gout_ref, hid_ref, br1_ref, n2_ref, act_ref, dg_ref, out_ref, gb2_ref, gb2s_ref, vec_ref, acc_ref):
    i = pl.program_id(0)

    @pl.when(i == 0)
    def _():
        br1 = nn(att_ref[...], wp_ref[...]) + bp_ref[...]
        br1_ref[...] = br1.astype(BF)
        hid = tok_ref[...] + sa_ref[...] * br1
        hid_ref[...] = hid
        unit, _ = unit_of(hid)
        n2_ref[...] = (unit * gain_ref[...] + bias_ref[...]).astype(BF)

    pre = nn(n2_ref[...], w1_ref[...]) + b1_ref[...]
    cdf = 0.5 + 0.5 * lax.erf(pre * INV_SQRT2)
    act = (pre * cdf).astype(BF)
    act_ref[...] = act
    dg_ref[...] = (cdf + pre * (jnp.exp(-0.5 * pre * pre) * INV_SQRT2PI)).astype(BF)
    part = nn(act, w2_ref[...])

    @pl.when(i == 0)
    def _():
        acc_ref[...] = part

    @pl.when(i > 0)
    def _():
        acc_ref[...] += part

    @pl.when(i == pl.num_programs(0) - 1)
    def _():
        br2 = acc_ref[...] + b2_ref[...]
        out_ref[...] = (hid_ref[...] + sm_ref[...] * br2).astype(BF)
        gout = gout_ref[...].astype(F32)
        gb2 = (sm_ref[...] * gout).astype(BF)
        gb2_ref[...] = gb2
        vec_ref[0:1, :] = jnp.sum(gout * br2, 0, keepdims=True)
        vec_ref[1:2, :] = jnp.sum(gb2.astype(F32), 0, keepdims=True)
        n = gb2s_ref.shape[1]
        gb2s_ref[...] = gb2_ref[:, pl.ds(pl.multiple_of((1 - order_ref[0]) * n, PAN), n)]


def mlp_fwd_call(order, att, tok, wp, bp, sa, gain, bias, w1, b1, w2, b2, sm, gout, tile=512):
    rows, width = tok.shape
    ff = w1.shape[1]
    mat, vec = whole((rows, width)), whole((1, width))
    col = pl.BlockSpec((rows, tile), lambda i, c: (0, i))
    return pl.pallas_call(
        mlp_fwd_body,
        grid_spec=pltpu.PrefetchScalarGridSpec(
            num_scalar_prefetch=1,
            grid=(ff // tile,),
            in_specs=[mat, mat, whole((width, width)), vec, vec, vec, vec,
                      pl.BlockSpec((width, tile), lambda i, c: (0, i)), pl.BlockSpec((1, tile), lambda i, c: (0, i)),
                      pl.BlockSpec((tile, width), lambda i, c: (i, 0)), vec, vec, mat],
            out_specs=[mat, mat, mat, col, col, mat, mat, whole((rows, width // 2)), whole((8, width))],
            scratch_shapes=[pltpu.VMEM((rows, width), F32)]),
        out_shape=[sd((rows, width), F32), sd((rows, width)), sd((rows, width)), sd((rows, ff)), sd((rows, ff)),
                   sd((rows, width)), sd((rows, width)), sd((rows, width // 2)), sd((8, width), F32)],
        compiler_params=params(56),
        cost_estimate=cost(rows * width * (2 * ff + width), 2 * (2 * width * ff + 2 * rows * ff + 6 * rows * width), rows * ff),
        name="mlp_fwd",
    )(order, att, tok, wp, bp, sa, gain, bias, w1, b1, w2, b2, sm, gout)


def mlp_bwd_body(half, order_ref, gb2_ref, dg_ref, w1_ref, w2_ref, hid_ref, br1_ref, gout_ref, wp_ref, sa_ref, gain_ref,
                 gpre_ref, gpres_ref, b1_ref, ghid_ref, gb1_ref, gb1s_ref, gatt_ref, vec_ref, acc_ref):
    i = pl.program_id(0)
    gpre = (nt(gb2_ref[...], w2_ref[...]) * dg_ref[...].astype(F32)).astype(BF)
    gpre_ref[...] = gpre

    @pl.when(i < half)
    def _():
        gpres_ref[...] = gpre

    b1_ref[0:1, :] = jnp.sum(gpre.astype(F32), 0, keepdims=True)
    part = nt(gpre, w1_ref[...])

    @pl.when(i == 0)
    def _():
        acc_ref[...] = part

    @pl.when(i > 0)
    def _():
        acc_ref[...] += part

    @pl.when(i == pl.num_programs(0) - 1)
    def _():
        unit, inv = unit_of(hid_ref[...])
        gn = acc_ref[...]
        vec_ref[0:1, :] = jnp.sum(gn * unit, 0, keepdims=True)
        vec_ref[1:2, :] = jnp.sum(gn, 0, keepdims=True)
        ghid = gout_ref[...].astype(F32) + unit_grad(gn * gain_ref[...], unit, inv)
        ghid_ref[...] = ghid
        vec_ref[2:3, :] = jnp.sum(ghid * br1_ref[...].astype(F32), 0, keepdims=True)
        gb1 = (sa_ref[...] * ghid).astype(BF)
        gb1_ref[...] = gb1
        vec_ref[3:4, :] = jnp.sum(gb1.astype(F32), 0, keepdims=True)
        n = gb1s_ref.shape[1]
        gb1s_ref[...] = gb1_ref[:, pl.ds(pl.multiple_of((1 - order_ref[0]) * n, PAN), n)]
        gatt_ref[...] = nt(gb1, wp_ref[...]).astype(BF)


def mlp_bwd_call(order, gb2, dg, w1, w2, hid, br1, gout, wp, sa, gain, tile=512):
    rows, width = hid.shape
    ff = w1.shape[1]
    steps = ff // tile
    half = steps // 2
    mat, vec, halfm = whole((rows, width)), whole((1, width)), whole((rows, width // 2))
    at = lambda i, c: (i + half * (1 - c[0])) % steps
    col = lambda n: pl.BlockSpec((n, tile), lambda i, c: (0, at(i, c)))
    return pl.pallas_call(
        functools.partial(mlp_bwd_body, half),
        grid_spec=pltpu.PrefetchScalarGridSpec(
            num_scalar_prefetch=1,
            grid=(steps,),
            in_specs=[mat, col(rows), col(width), pl.BlockSpec((tile, width), lambda i, c: (at(i, c), 0)),
                      mat, mat, mat, whole((width, width)), vec, vec],
            out_specs=[col(rows), pl.BlockSpec((rows, tile), lambda i, c: (0, jnp.minimum(i, half - 1))), col(8),
                       mat, mat, halfm, mat, whole((8, width))],
            scratch_shapes=[pltpu.VMEM((rows, width), F32)]),
        out_shape=[sd((rows, ff)), sd((rows, ff // 2)), sd((8, ff), F32), sd((rows, width), F32), sd((rows, width)),
                   sd((rows, width // 2)), sd((rows, width)), sd((8, width), F32)],
        compiler_params=params(56),
        cost_estimate=cost(rows * width * (2 * ff + width), 2 * (2 * width * ff + 2 * rows * ff + 6 * rows * width)),
        name="mlp_bwd",
    )(order, gb2, dg, w1, w2, hid, br1, gout, wp, sa, gain)


def put_panels(ref, lead, base, value, rows):
    n = value.shape[1] // PAN
    for chip, place in enumerate(lead):
        for rg in range(rows // 16):
            for pc in range(n):
                r0 = chip * rows + rg * 16
                ref[(0,) + place + (base + rg * n + pc,)] = value[r0:r0 + 16, pc * PAN:(pc + 1) * PAN]


CHIPS_OF_Z = list(itertools.product(range(2), range(4), range(2)))


def vector_panels(vec_refs, wide_refs):
    r = lax.broadcasted_iota(jnp.int32, (256, 1), 0)
    device = jnp.where(r % 16 < 2, r // 16 * 2 + r % 16, -1)
    total, at = None, 0
    for ref, row, per in [(v, i, 8) for v, rows in vec_refs for i in rows] + wide_refs:
        n = 32 * per
        lane = lax.broadcasted_iota(jnp.int32, (1, n), 1)
        spread = jnp.where(lane // per == device, ref[row:row + 1, :], 0.0).astype(BF)
        pick_r = lax.broadcasted_iota(jnp.int32, (n, PAN), 0)
        pick_c = lax.broadcasted_iota(jnp.int32, (n, PAN), 1)
        part = nn(spread, jnp.where(pick_r % per + at == pick_c, 1.0, 0.0).astype(BF))
        total = part if total is None else total + part
        at += per
    return total.astype(BF)


def dw_near_body(jobs, extra, order_ref, *refs):
    send_ref, keep_ref = refs[-2:]
    i = pl.program_id(0)
    done, at, base = [], 0, 0
    for rows, panels in jobs:
        a0, a1, g0, g1 = (ref[...] for ref in refs[at:at + 4])
        done.append(((tn(a0, g0) + tn(a1, g1)).astype(BF), base, rows))
        at, base = at + 4, base + panels
    if extra:
        pos_ref, vf, vb, vt, b1, qv = refs[at:at + 6]
        done.append((vector_panels([(vf, (0, 1)), (vb, (0, 1, 2, 3)), (vt, (0, 1, 2))], [(b1, 0, 32), (qv, 0, 16)]),
                     base + 4, 16))

    def write(ref):
        for value, first, rows in done:
            put_panels(ref, CHIPS_OF_Z, first, value, rows)
        if extra:
            half = pos_ref.shape[1] // 2
            for yh, x, side, rg, pc in itertools.product(range(2), range(4), range(2), range(2), range(2)):
                r0, c0 = (yh * 4 + x) * 32 + rg * 16, side * half + pc * PAN
                yl = order_ref[9] if side == 0 else 1 - order_ref[9]
                ref[0, yh, x, yl, base + rg * 2 + pc] = pos_ref[r0:r0 + 16, c0:c0 + PAN]

    pl.when(i < 2)(lambda: write(send_ref))
    pl.when(i >= 2)(lambda: write(keep_ref))


def dw_near_call(order, jobs, extra=()):
    ins, args, shapes, macs = [], [], [], 0
    for a0, a1, g0, g1 in jobs:
        rows, k = a0.shape
        n = g0.shape[1]
        lhs = pl.BlockSpec((rows, k // 4), lambda i, c: (0, c[1 + i]))
        ins += [lhs, lhs, whole((rows, n)), whole((rows, n))]
        args += [a0, a1, g0, g1]
        shapes.append((k // 64, k // 1024 * (n // PAN)))
        macs += 2 * rows * k * n
    panels = sum(p for _, p in shapes)
    if extra:
        pos, *vecs = extra
        ins.append(pl.BlockSpec((pos.shape[0] // 4, pos.shape[1]), lambda i, c: (c[1 + i], 0)))
        ins += [pl.BlockSpec((8, v.shape[1] // 4), lambda i, c: (0, c[1 + i])) for v in vecs]
        args += list(extra)
        panels += 5
    block = (1, 2, 4, 2, panels, 16, PAN)
    out = sd((2,) + block[1:])
    at = lambda f: pl.BlockSpec(block, lambda i, c: (f(i),) + (0,) * 6)
    return pl.pallas_call(
        functools.partial(dw_near_body, tuple(shapes), bool(extra)),
        grid_spec=pltpu.PrefetchScalarGridSpec(
            num_scalar_prefetch=1, grid=(4,), in_specs=ins,
            out_specs=[at(lambda i: jnp.minimum(i, 1)), at(lambda i: jnp.maximum(i - 2, 0))]),
        out_shape=[out, out],
        compiler_params=params(48),
        cost_estimate=cost(macs, 2 * sum(a.size for a in args) + 4 * out.size),
        name="dw_near",
    )(order, *args)


def dw_far_body(order_ref, a0_ref, a1_ref, g0_ref, g1_ref, send_ref, keep_ref):
    i = pl.program_id(0)
    n = g1_ref.shape[1] // PAN
    total = (tn(a0_ref[...], g0_ref[...]) + tn(a1_ref[...], g1_ref[...])).astype(BF)
    for target in range(4):
        at = order_ref[5 + target]

        def write(ref, slot):
            for yh, yl, pc in itertools.product(range(2), range(2), range(n)):
                r0 = (yh * 4 + target) * 32 + yl * 16
                ref[slot, i, yh, yl, pc] = total[r0:r0 + 16, pc * PAN:(pc + 1) * PAN]

        pl.when(at < 2)(functools.partial(write, send_ref, at))
        pl.when(at >= 2)(functools.partial(write, keep_ref, at - 2))


def dw_far_call(order, a0, a1, g0, g1):
    rows, k = a0.shape
    nh = g1.shape[1]
    lhs = pl.BlockSpec((rows, k // 4), lambda i, c: (0, i))
    shape = (2, 4, 2, 2, nh // PAN, 16, PAN)
    return pl.pallas_call(
        dw_far_body,
        grid_spec=pltpu.PrefetchScalarGridSpec(
            num_scalar_prefetch=1,
            grid=(4,),
            in_specs=[lhs, lhs, pl.BlockSpec((rows, nh), lambda i, c: (0, c[0])), whole((rows, nh))],
            out_specs=[whole(shape), whole(shape)]),
        out_shape=[sd(shape)] * 2,
        compiler_params=params(48),
        cost_estimate=cost(2 * rows * k * nh, 2 * (2 * rows * k + 2 * rows * nh + k * nh)),
        name="dw_far",
    )(order, a0, a1, g0, g1)


def tok_bwd_body(half, order_ref, g_mine0, g_mine1, g_send0, g_send1, wq_ref, wk_ref, wv_ref, tok_ref, ghid_ref, gain_ref,
                 mask_ref, own_ref, send_ref, pos_ref, cls_ref, vec_ref, qv_ref, acc_ref):
    i = pl.program_id(0)
    n = wq_ref.shape[1]
    width = tok_ref.shape[1]
    core = order_ref[0]
    for step, g_ref in enumerate((g_mine0, g_mine1, g_send0, g_send1)):
        @pl.when(i == step)
        def _():
            part = nt(g_ref[:, 0:n], wq_ref[...]) + nt(g_ref[:, n:2 * n], wk_ref[...]) + nt(g_ref[:, 2 * n:], wv_ref[...])
            if step == 0:
                acc_ref[...] = part
            else:
                acc_ref[...] += part
            sums = jnp.sum(g_ref[...].astype(F32), 0, keepdims=True)
            side = core if step < 2 else 1 - core
            at = pl.multiple_of((step % 2) * 2 * n + side * n, PAN)
            qv_ref[0:1, pl.ds(at, n)] = sums[:, 0:n]
            qv_ref[0:1, pl.ds(width + at, n)] = sums[:, 2 * n:]

    @pl.when(i == 3)
    def _():
        unit, inv = unit_of(tok_ref[...])
        gn = acc_ref[...]
        vec_ref[0:1, :] = jnp.sum(gn * unit, 0, keepdims=True)
        vec_ref[1:2, :] = jnp.sum(gn, 0, keepdims=True)
        gtok = ghid_ref[...] + unit_grad(gn * gain_ref[...], unit, inv)
        vec_ref[2:3, :] = jnp.sum(gtok * mask_ref[:, 0:1].astype(F32), 0, keepdims=True)
        own_ref[...] = gtok[0:half]
        send_ref[...] = gtok[half:].astype(BF)
        cls_ref[...] = gtok[2 * half:2 * half + 8]
        pos_ref[...] = gtok[0:2 * half].T.astype(BF)


def tok_bwd_call(order, mine, send, w, tok, ghid, gain, mask):
    rows, width = tok.shape
    half = (rows - TAIL) // 2
    n = mine[0].shape[1] // 3
    per = width // n
    mat, vec = whole((rows, width)), whole((1, width))
    gs = whole((rows, 3 * n))
    head = lambda i, c: (i % 2) * 2 + jnp.where(i < 2, c[0], 1 - c[0])
    ws = [pl.BlockSpec((width, n), lambda i, c, j=j: (0, j * per + head(i, c))) for j in range(3)]
    return pl.pallas_call(
        functools.partial(tok_bwd_body, half),
        grid_spec=pltpu.PrefetchScalarGridSpec(
            num_scalar_prefetch=1,
            grid=(4,),
            in_specs=[gs] * 4 + ws + [mat, mat, vec, whole((rows, PAN))],
            out_specs=[whole((half, width)), whole((half + TAIL, width)), whole((width, 2 * half)), whole((8, width)),
                       whole((8, width)), whole((8, 2 * width))],
            scratch_shapes=[pltpu.VMEM((rows, width), F32)]),
        out_shape=[sd((half, width), F32), sd((half + TAIL, width)), sd((width, 2 * half)), sd((8, width), F32),
                   sd((8, width), F32), sd((8, 2 * width), F32)],
        compiler_params=params(48),
        cost_estimate=cost(rows * width * 3 * width, 2 * (3 * width * width + 8 * rows * width)),
        name="tok_bwd",
    )(order, *mine, *send, w, w, w, tok, ghid, gain, mask)


def near_sum_body(keep_ref, came_ref, kept_ref, send_ref):
    kept_ref[...] = keep_ref[0].astype(F32) + came_ref[0].astype(F32)
    send_ref[...] = (keep_ref[1].astype(F32) + came_ref[1].astype(F32)).astype(BF)


def near_sum(keep, came, parts=4):
    shape = keep.shape
    m = keep.size // (2 * 16 * PAN)
    flat = lambda a: a.reshape(2, m, 16, PAN)
    parts = parts if m % parts == 0 and m >= 16 else 1
    two = pl.BlockSpec((2, m // parts, 16, PAN), lambda i: (0, i, 0, 0))
    one = pl.BlockSpec((m // parts, 16, PAN), lambda i: (i, 0, 0))
    kept, send = pl.pallas_call(
        near_sum_body, grid=(parts,), in_specs=[two, two], out_specs=[one, one],
        out_shape=[sd((m, 16, PAN), F32), sd((m, 16, PAN))],
        compiler_params=params(24), cost_estimate=cost(0, keep.size * 6), name="near_sum",
    )(flat(keep), flat(came))
    return kept.reshape(shape[1:]), send.reshape(shape[1:])


def far_sum_body(axis, count, order_ref, *refs):
    send_ref, keep_ref = refs[-2:]
    for slot in range(4):
        target = order_ref[1 + slot]
        at = 0
        for j in range(count):
            keep, came = refs[2 * j], refs[2 * j + 1]
            n = keep.shape[-3]
            if axis == "y":
                where = (target // 2, target % 2)
            elif axis == "z":
                where = (target,)
            else:
                where = (slice(None), target)
            total = keep[where].astype(F32) + came[where].astype(F32)
            out = (slot % 2,) + (slice(None),) * (total.ndim - 3) + (slice(at, at + n),)
            if slot < 2:
                send_ref[out] = total.astype(BF)
            else:
                keep_ref[out] = total
            at += n


def far_sum(order, pairs, axis):
    lead = {"z": 1, "x": 2, "y": 2}[axis]
    shape = pairs[0][0].shape
    rest = ((shape[0],) if axis == "x" else ()) + shape[lead:-3]
    panels = sum(k.shape[-3] for k, _ in pairs)
    out = (2,) + rest + (panels, 16, PAN)
    args = [a for pair in pairs for a in pair]
    return pl.pallas_call(
        functools.partial(far_sum_body, axis, len(pairs)),
        grid_spec=pltpu.PrefetchScalarGridSpec(
            num_scalar_prefetch=1, grid=(1,),
            in_specs=[whole(a.shape) for a in args],
            out_specs=[whole(out)] * 2),
        out_shape=[sd(out), sd(out, F32)],
        compiler_params=params(40), cost_estimate=cost(0, sum(a.size for a in args) * 6), name="far_sum",
    )(order, *args)


def last_sum_body(order_ref, keep_ref, came_ref, cls_ref, mine_ref, gone_ref, pos_ref, tot_ref):
    core = order_ref[0]
    tot_ref[...] = keep_ref[...] + came_ref[...].astype(F32)
    at = 0

    def put(panel, start):
        nonlocal at
        for ref, side in ((mine_ref, core), (gone_ref, 1 - core)):
            ref[at] = tot_ref[panel, pl.ds(pl.multiple_of(start(side), 8), 8), :]
        at += 1

    for rg, pc, part in itertools.product(range(2), range(4), range(2)):
        for ref, side in ((mine_ref, core), (gone_ref, 1 - core)):
            ref[at] = tot_ref[(2 * side + rg) * 4 + pc, 8 * part:8 * part + 8, :]
        at += 1
    for panel in list(range(16, 42)):
        if panel < 42:
            put(panel, lambda side: side * 8)
    for panel in range(42, 48):
        put(panel, lambda side: side * 8)
    mine_ref[at] = tot_ref[52, 0:8, :]
    gone_ref[at] = tot_ref[52, 0:8, :]
    for part in range(2):
        mine_ref[at + 1 + part] = cls_ref[8 * part:8 * part + 8, :]
        gone_ref[at + 1 + part] = cls_ref[8 * part:8 * part + 8, :]
    for rg, pc in itertools.product(range(2), range(2)):
        pos_ref[16 * rg:16 * rg + 16, pc * PAN:(pc + 1) * PAN] = tot_ref[48 + rg * 2 + pc]


SWAPPED = 16 + 26 + 6 + 3


def last_sum(order, keep, came, cls16):
    shape = sd((SWAPPED, 8, PAN), F32)
    return pl.pallas_call(
        last_sum_body,
        grid_spec=pltpu.PrefetchScalarGridSpec(
            num_scalar_prefetch=1, grid=(1,),
            in_specs=[whole(keep.shape), whole(came.shape), whole(cls16.shape)],
            out_specs=[whole(shape.shape), whole(shape.shape), whole((32, 256))],
            scratch_shapes=[pltpu.VMEM(keep.shape, F32)]),
        out_shape=[shape, shape, sd((32, 256), F32)],
        compiler_params=params(24), cost_estimate=cost(0, keep.size * 10), name="last_sum",
    )(order, keep, came, cls16)


def finish_body(order_ref, mine_ref, came_ref, fc2_ref, fc1_ref, proj_ref, qkv_ref, vec_ref, cls_ref):
    first = order_ref[0] == 0
    at = 0

    def halves():
        nonlocal at
        mine, came = mine_ref[at], came_ref[at]
        at += 1
        return jnp.where(first, mine, came), jnp.where(first, came, mine)

    for rg, pc, part in itertools.product(range(2), range(4), range(2)):
        r0 = rg * 16 + part * 8
        for h, value in enumerate(halves()):
            fc2_ref[r0:r0 + 8, 512 * h + pc * PAN:512 * h + (pc + 1) * PAN] = value
    for pc in range(16):
        for h, value in enumerate(halves()):
            fc1_ref[:, 2048 * h + pc * PAN:2048 * h + (pc + 1) * PAN] = value
    for pc in range(4):
        for h, value in enumerate(halves()):
            proj_ref[:, 512 * h + pc * PAN:512 * h + (pc + 1) * PAN] = value
    for group, kind, pc in itertools.product(range(2), range(3), range(2)):
        for h, value in enumerate(halves()):
            c0 = kind * 1024 + group * 512 + h * 256 + pc * PAN
            qkv_ref[:, c0:c0 + PAN] = value
    vec_ref[...] = mine_ref[at] + came_ref[at]
    for part in range(2):
        cls_ref[8 * part:8 * part + 8, :] = mine_ref[at + 1 + part] + came_ref[at + 1 + part]


def finish(order, mine, came):
    outs = [(32, 1024), (8, 4096), (8, 1024), (8, 3072), (8, PAN), (16, PAN)]
    return pl.pallas_call(
        finish_body,
        grid_spec=pltpu.PrefetchScalarGridSpec(
            num_scalar_prefetch=1, grid=(1,), in_specs=[whole(mine.shape)] * 2, out_specs=[whole(s) for s in outs]),
        out_shape=[sd(s, F32) for s in outs],
        compiler_params=params(24), cost_estimate=cost(0, mine.size * 16), name="finish",
    )(order, mine, came)


def swap(x, axis):
    return lax.ppermute(x, axis, [(0, 1), (1, 0)])


def after(x, *others):
    return lax.optimization_barrier((x,) + others)[0]


def partners(axis, turn):
    pairs = []
    for z, yh, x, yl, core in itertools.product(*(range(SIZES[a]) for a in ALL)):
        at = {"z": z, "y": yh * 2 + yl, "x": x}
        flat = lambda p: (((p["z"] * 2 + p["y"] // 2) * 4 + p["x"]) * 2 + p["y"] % 2) * 2 + core
        there = dict(at)
        there[axis] ^= 1 if core == turn else 3
        pairs.append((flat(at), flat(there)))
    return pairs


def pass_on(x, axis, turn):
    return lax.ppermute(x, ALL, partners(axis, turn))


def order_of(axis):
    me = lax.axis_index("yh") * 2 + lax.axis_index("yl") if axis == "y" else lax.axis_index(axis)
    first = jnp.where(lax.axis_index("core") == 0, 1, 3)
    targets = [me ^ first, me ^ 2, me, me ^ first ^ 2]
    places = [sum(jnp.where(t == want, at, 0) for at, t in enumerate(targets)) for want in range(4)]
    return jnp.stack([lax.axis_index("core")] + targets + places + [lax.axis_index("yl")]).astype(jnp.int32)


class Scatter:
    def __init__(self, orders, send, keep, axis):
        self.orders, self.axis, self.keep = orders, axis, keep
        self.came = pass_on(send, axis, 0)

    def near(self):
        self.kept, send = near_sum(self.keep, self.came)
        self.came = pass_on(send, self.axis, 1)
        return send

    def far(self, axis, *others):
        pairs = [(s.kept, s.came) for s in (self,) + others]
        send, self.keep = far_sum(self.orders[axis], pairs, axis)
        self.axis = axis
        self.came = pass_on(send, axis, 0)
        return send


def local(patches, cls_tokens, patch_masks, mask_token, pos_embed, ln1_gain, ln1_bias, qkv_weight, qv_bias, proj_weight,
          proj_bias, scale_attn, ln2_gain, ln2_bias, fc1_weight, fc1_bias, fc2_weight, fc2_bias, scale_mlp, cot_patches,
          cot_cls):
    half, _, width = patches.shape
    pairs = 4
    core, yl = lax.axis_index("core"), lax.axis_index("yl")
    row = lambda v: v.reshape(1, -1)
    sides = lambda a: (jnp.where(yl == 0, a[:, 0], a[:, 1]), jnp.where(yl == 0, a[:, 1], a[:, 0]))
    both = lambda mine, other, axis: jnp.where(yl == 0, jnp.stack((mine, other), axis), jnp.stack((other, mine), axis))
    pad = jnp.zeros((TAIL - 1, width), BF)
    orders = {a: order_of(a) for a in "zxy"}
    order = orders["z"]

    mask_f = patch_masks.astype(F32)
    mask3 = patch_masks[..., None]
    mixed = jnp.where(mask3 != 0, mask_token, patches)
    own, send = sides(mixed)
    came = swap(send, "yl")
    pos_came = lax.ppermute(pos_embed, Y, [(0, 3), (3, 0), (1, 2), (2, 1)])
    cls_row = jnp.where(yl == 0, cls_tokens[0:1], cls_tokens[1:2])
    tok = jnp.concatenate((own.astype(F32) + pos_embed.astype(F32), came.astype(F32) + pos_came.astype(F32),
                           cls_row.astype(F32), pad.astype(F32)), 0)

    add = row(jnp.concatenate((qv_bias[:width], jnp.zeros((width,), F32), qv_bias[width:])))
    n1, kv0 = project_call(tok, qkv_weight, add, 2, 2, norm=(row(ln1_gain), row(ln1_bias)))
    kv0_p = swap(kv0, "core")
    kv1 = project_call(after(n1, kv0), qkv_weight, add, 3, 2)
    kv1_p = swap(after(kv1, kv0_p), "core")
    q = project_call(after(n1, kv1), qkv_weight, add, 0, 1, scale=0.125)

    mask_own, mask_send = sides(mask_f)
    cot_own, cot_send = sides(jnp.where(mask3 != 0, cot_patches, jnp.zeros_like(cot_patches)))
    lanes = lambda m: jnp.broadcast_to(m.astype(BF)[:, None], (half, PAN))
    cot_came = swap(after(jnp.concatenate((cot_send, lanes(mask_send)), 1), came), "yl")

    att, lse0 = att_fwd_call(q, kv0, kv0_p, 0, pairs)
    att, lse1 = att_fwd_call(q, kv1, kv1_p, 1, pairs, into=att)
    n1_p = swap(after(n1, kv1_p), "core")
    cot_came = after(cot_came, att)
    cls_cot = jnp.where(yl == 0, cot_cls[0:1], cot_cls[1:2]) * (core == 0).astype(BF)
    gout = jnp.concatenate((cot_own, cot_came[:, :width], cls_cot, pad), 0)
    mask_rows = jnp.concatenate((lanes(mask_own), cot_came[:, width:], jnp.zeros((TAIL, PAN), BF)), 0)
    hid, br1, n2, act, dg, out, gb2, gb2_send, vec_f = mlp_fwd_call(
        order, att, tok, proj_weight, row(proj_bias), row(scale_attn), row(ln2_gain), row(ln2_bias), fc1_weight,
        row(fc1_bias), fc2_weight, row(fc2_bias), row(scale_mlp), gout)
    gb2_p = swap(gb2_send, "core")
    act_p = swap(after(act, gb2_p), "core")
    mine_half = lambda g: lax.dynamic_slice_in_dim(g, core * (g.shape[1] // 2), g.shape[1] // 2, 1)
    att_p = swap(after(att, act_p), "core")
    n2_p = swap(after(n2, att_p), "core")
    out_came = swap(out[half:], "yl")

    send, keep = dw_near_call(order, [(act, act_p, mine_half(gb2), gb2_p)])
    fc2 = Scatter(orders, send, keep, "z")
    gpre, gpre_send, fc1_vec, ghid, gb1, gb1_send, gatt, vec_b = mlp_bwd_call(
        order, after(gb2, send), dg, fc1_weight, fc2_weight, hid, br1, gout, proj_weight, row(scale_attn), row(ln2_gain))
    gpre_p = swap(gpre_send, "core")
    gb1_p = swap(after(gb1_send, gpre_p), "core")
    done = fc2.near()
    send, keep = dw_far_call(orders["x"], after(n2, done), n2_p, gpre, gpre_p)
    fc1 = Scatter(orders, send, keep, "x")
    dq, dkv, part = att_bwd_call(q, kv0, kv0_p, after(gatt, send), att, lse0, 0, pairs)
    mine0, send0 = trip_call(order, dq, dkv, swap(part, "core"))
    done1, done2 = fc1.near(), fc2.far("x")
    trip0 = swap(send0, "core")
    dq, dkv, part = att_bwd_call(q, kv1, kv1_p, after(gatt, send0, done1, done2), att, lse1, 1, pairs)
    came1 = swap(part, "core")
    done1, done2 = fc1.far("z"), fc2.near()
    send, keep = dw_near_call(order, [(att, att_p, mine_half(gb1), gb1_p), (after(n1, done1, done2, dq), n1_p, mine0, trip0)])
    mid = Scatter(orders, send, keep, "z")
    mine1, send1 = trip_call(order, dq, dkv, after(came1, send))
    trip1 = swap(send1, "core")
    own, gtok_send, pos, cls8, vec_t, qv = tok_bwd_call(
        order, (mine0, mine1), (send0, send1), qkv_weight, tok, ghid, row(ln1_gain), mask_rows)
    gtok_came = swap(gtok_send, "yl")
    send, keep = dw_near_call(order, [(after(n1, pos), n1_p, mine1, trip1)], extra=(pos, vec_f, vec_b, vec_t, fc1_vec, qv))
    end = Scatter(orders, send, keep, "z")
    fc1.near(), mid.near(), end.near()
    mid.far("x"), end.far("x")
    mid.near(), end.near()
    fc2.far("y", fc1, mid, end)
    fc2.near()

    gtok_came = gtok_came.astype(F32)
    grad_patches = both(own, gtok_came[:half], 1) * (1.0 - mask_f[..., None])
    cls_part = both(cls8[0], gtok_came[half], 0)
    gone = (order, fc2.kept, fc2.came, cls_part.reshape(16, PAN))
    mine, gone, grad_pos = last_sum(*gone)
    fc2_g, fc1_g, proj_g, qkv_g, vec8, cls16 = finish(order, mine, swap(gone, "core"))
    sums = lax.dynamic_index_in_dim(vec8, core, 0, False)
    v = [sums[8 * j:8 * j + 8] for j in range(9)] + [sums[72:104], sums[104:120]]
    out_came = after(out_came, gtok_send)
    out_patches = both(out[:half], out_came[:half], 1)
    out_cls = both(out[2 * half], out_came[half], 0)
    return (out_patches, out_cls, grad_patches, cls16.reshape(2, width), v[8], grad_pos.T, v[6], v[7], qkv_g, v[10],
            proj_g, v[5], v[4], v[2], v[3], fc1_g, v[9], fc2_g, v[1], v[0])


def solution(mesh):
    fine = Mesh(mesh.devices.reshape([SIZES[a] for a in ALL]), ALL)
    img, blk = ("z", "yh", "x"), ("yl", "core")
    every = img + blk
    rep, crops, rows = P(), P(img, None), P(blk, img, None)
    vec, mat = P(every), P(every, None)
    return jax.shard_map(
        local,
        mesh=fine,
        in_specs=(rows, crops, P(blk, img), rep, P(blk, None)) + (rep,) * 14 + (rows, crops),
        out_specs=(rows, crops, rows, crops, vec, P(blk, img), vec, vec, mat, vec, mat, vec, vec, vec, vec, mat, vec, mat,
                   vec, vec),
        check_vma=False,
    )
```

time: 1660 us -> 383 us (0.23)
  waiting for transfers between devices: 756 us -> 98.7 us
  local copies, waits for them, and re-layouts: 413 us -> 28.5 us
  matrix products: 255 us -> 0 us
  Pallas kernels: 0 us -> 190 us
  other arithmetic: 186 us -> 11.4 us
  starting transfers between devices: 18 us -> 46.1 us
    unnamed x6 -> x0, waiting for transfers between devices: 697 us -> none
    dot_general x44 -> x0, matrix products: 255 us -> none  [the longest x8 56.9 us: dot_outer(): lax.dot_general(left, right, (((0,), (0,)), ((), ())), preferred_element_...]
    unnamed x358 -> x98, local copies, waits for them, and re-layouts: 210 us -> 16.3 us
    pallas_call x0 -> x32, Pallas kernels: none -> 190 us  [the longest x2 32.6 us: att_bwd_call(): pl.pallas_call(functools.partial(att_bwd_body, np_), grid=(pairs,), in_sp...]
    ppermute x0 -> x37, waiting for transfers between devices: none -> 98.7 us  [the longest x18 77.1 us: pass_on(): return lax.ppermute(x, ALL, partners(axis, turn))]
    mul x4 -> x2, other arithmetic: 60.9 us -> 0.27 us  [the longest x1 0.25 us: local(): grad_patches = both(own, gtok_came[:half], 1) * (1.0 - mask_f[..., None])]
    reduce_sum x15 -> x0, other arithmetic: 60 us -> none  [the longest x2 36.6 us: local(): inner = jnp.sum(probs_back * g_probs, -1, keepdims=True)]
    another operation x20 -> x6, local copies, waits for them, and re-layouts: 58 us -> 3.02 us  [the longest x3 2.25 us: local(): jnp.stack((mine, other), axis)]
  transfers between devices with their start and end apart: 8 -> 37, of which waited for: 6 -> 14; matrix products, arithmetic and copies ran while one was open for 13% -> 5% of each run, Pallas kernels for 0% -> 36%
where the time goes in v1:
time: 383 us; the launch traced here: 376 us
  Pallas kernels  190 us (50%)
  waiting for transfers between devices  98.7 us (26%)
  starting transfers between devices  46.1 us (12%)
  local copies, waits for them, and re-layouts  28.5 us (7%)
  other arithmetic  11.4 us (3%)
    ppermute x18, waiting for transfers between devices, pass_on(): return lax.ppermute(x, ALL, partners(axis, turn))  77.1 us
    pallas_call x2, Pallas kernels, att_bwd_call(): pl.pallas_call(functools.partial(att_bwd_body, np_), grid=(pairs,), in_sp...  32.6 us
    ppermute x18, starting transfers between devices, pass_on(): return lax.ppermute(x, ALL, partners(axis, turn))  31.3 us
    pallas_call x3, Pallas kernels, dw_near_call(): pl.pallas_call(functools.partial(dw_near_body, tuple(shapes), bool(extra)...  29 us
    pallas_call x1, Pallas kernels, mlp_bwd_call(): pl.pallas_call(functools.partial(mlp_bwd_body, half), grid_spec=pltpu.Pre...  26.1 us
    pallas_call x1, Pallas kernels, mlp_fwd_call(): pl.pallas_call(mlp_fwd_body, grid_spec=pltpu.PrefetchScalarGridSpec(num_s...  25.9 us
    pallas_call x2, Pallas kernels, att_fwd_call(): pl.pallas_call(functools.partial(att_fwd_body, np_, chunk=chunk), grid=(p...  21.5 us
    ppermute x18, waiting for transfers between devices, swap(): return lax.ppermute(x, axis, [(0, 1), (1, 0)])  19 us
  transfers between devices with their start and end apart: 37, of which 14 were waited for; matrix products, arithmetic and copies ran while one was open for 5% of the time, Pallas kernels for 36%

profile of v1, /device:TPU:0, one launch (start us, length us, event | category | flops | bytes accessed | tf_op | source)
XLA Modules:
  0.0 376.2 jit_solution(506327954354452734)
XLA Ops:
  1.4 3.4 copy_select_fusion
  4.8 1.7 collective-permute-start
  6.5 2.2 collective-permute-start.1
  9.1 9.3 %collective-permute-done = bf16[256,1024]{1,0:T(8,128)(2,1)S(1)} collective-permute-done((bf16[256,1024]{1,0:T(8,128)(2,1)S(1)}, bf16[256,1024]{1,0:T(8,128)(2,1)S(1)}, u32[]{:S(2)}, u32[]{:S(2)}) %collective-permute-start) | collective-permute-done | bytes 524320 | tf_op jit(solution)/shard_map/ppermute | solution.py:694
  18.5 2.7 collective-permute-done.1
  22.0 2.4 norm_project.1
  24.5 1.7 project.2.ko_ref.vo_ref
  28.5 2.1 select_bitcast_fusion.1
  32.6 2.8 copy-done
  35.3 1.7 project.3.q_ref
  37.1 10.7 %att_fwd.2 = (bf16[528,1024]{1,0:T(8,128)(2,1)S(1)}, f32[528,512]{1,0:T(8,128)S(1)}) custom-call(bf16[528,1024]{1,0:T(8,128)(2,1)S(1)} %project.3.q_ref, bf16[528,1024]{1,0:T(8,128)(2,1)S(1)} %copy-done.20, bf16[528,1024]{1,0:T(8,128)(2,1)S(1)} %copy-done.20, bf16[528,1024]{1,0:T(8,128)(2,1)S(1)} %copy-done.23, bf16[528,1024]{1,0:T(8,128)(2,1)S(1)} %copy-done.23), custom_call_target="tpu_custom_call" | custom-call | flops 2214592512 | bytes 4325376 | tf_op jit(solution)/shard_map/att_fwd/pallas_call | solution.py:130
  47.9 10.7 %att_fwd.3 = (bf16[528,1024]{1,0:T(8,128)(2,1)S(1)}, f32[528,512]{1,0:T(8,128)S(1)}) custom-call(bf16[528,1024]{1,0:T(8,128)(2,1)S(1)} %project.3.q_ref, bf16[528,1024]{1,0:T(8,128)(2,1)S(1)} %project.2.ko_ref.vo_ref, bf16[528,1024]{1,0:T(8,128)(2,1)S(1)} %project.2.ko_ref.vo_ref, ...), custom_call_target="tpu_custom_call", output_to_operand_aliasing={{0}: (5, {})} | custom-call | flops 2214592512 | bytes 4325376 | tf_op jit(solution)/shard_map/att_fwd/pallas_call | solution.py:130
  58.7 1.5 slice.148
  60.2 1.3 maximum_maximum_fusion.1.gout_ref
  61.4 25.9 %mlp_fwd.1 = (f32[528,1024]{1,0:T(8,128)}, bf16[528,1024]{1,0:T(8,128)(2,1)}, bf16[528,1024]{1,0:T(8,128)(2,1)}, bf16[528,4096]{1,0:T(8,128)(2,1)}, bf16[528,409...) custom-call(s32[10]{0:T(128)} %stack.141.order_ref, ...), custom_call_target="tpu_custom_call" | custom-call | flops 9965666304 | bytes 31916032 | tf_op jit(solution)/shard_map/mlp_fwd/pallas_call | solution.py:282
  87.8 1.8 collective-permute-done.6.refs_3_
  91.8 6.2 %collective-permute-done.7.refs_1_ = bf16[528,4096]{1,0:T(8,128)(2,1)} collective-permute-done((bf16[528,4096]{1,0:T(8,128)(2,1)}, bf16[528,4096]{1,0:T(8,128)(2,1)}, u32[]{:S(2)}, u32[]{:S(2)}) %collective-permute-start.7) | collective-permute-done | bytes 4325408 | tf_op jit(solution)/shard_map/ppermute | solution.py:694
  100.0 11.0 %dw_near.3 = (bf16[2,2,4,2,16,16,128]{6,5,4,3,2,1,0:T(8,128)(2,1)}, bf16[2,2,4,2,16,16,128]{6,5,4,3,2,1,0:T(8,128)(2,1)S(1)}) custom-call(s32[10]{0:T(128)S(1)} %copy-done.13, bf16[528,4096]{1,0:T(8,128)(2,1)} %get-tuple-element.134.refs_0_, bf16[528,4096]{1,0:T(8,128)(2,1)} %collective-permute-done.7.refs_1_, ...), custom_call_target="tpu_custom_call" | custom-call | flops 4429185024 | bytes 13926400 | tf_op jit(solution)/shard_map/dw_near/pallas_call | solution.py:439
  110.9 26.1 %mlp_bwd.1 = (bf16[528,4096]{1,0:T(8,128)(2,1)}, bf16[528,2048]{1,0:T(8,128)(2,1)}, f32[8,4096]{1,0:T(8,128)}, f32[528,1024]{1,0:T(8,128)}, bf16[528,1024]{1,0:T...) custom-call(s32[10]{0:T(128)} %stack.141.order_ref, ...), custom_call_target="tpu_custom_call" | custom-call | flops 9965666304 | bytes 31916032 | tf_op jit(solution)/shard_map/mlp_bwd/pallas_call | solution.py:346
  137.2 1.9 collective-permute-start.8
  140.2 2.2 collective-permute-start.10
  142.5 21.1 %collective-permute-done.8 = bf16[2,2,4,2,16,16,128]{6,5,4,3,2,1,0:T(8,128)(2,1)} collective-permute-done((bf16[2,2,4,2,16,16,128]{6,5,4,3,2,1,0:T(8,128)(2,1)}, bf16[2,2,4,2,16,16,128]{6,5,4,3,2,1,0:T(8,128)(2,1)}, u32[]{:S(2)}, u32[]{:S(2)}) %collective-permute-start.8) | collective-permute-done | bytes 2097184 | tf_op jit(solution)/shard_map/ppermute | solution.py:713
  163.6 3.7 near_sum.9
  167.4 13.2 %dw_far.1 = (bf16[2,4,2,2,16,16,128]{6,5,4,3,2,1,0:T(8,128)(2,1)}, bf16[2,4,2,2,16,16,128]{6,5,4,3,2,1,0:T(8,128)(2,1)}) custom-call(s32[10]{0:T(128)S(1)} %stack.151.order_ref, bf16[528,1024]{1,0:T(8,128)(2,1)} %get-tuple-element.146.a0_ref, bf16[528,1024]{1,0:T(8,128)(2,1)} %collective-permute-done.10.a1_ref, bf16[528,4096]{1,0:T(8,128)(2,1)} %get-tuple-element.147.g0_ref, ...), custom_call_target="tpu_custom_call" | custom-call | flops 4429185024 | bytes 10682368 | tf_op jit(solution)/shard_map/dw_far/pallas_call | solution.py:472
  180.6 1.5 collective-permute-start.13
  182.1 4.2 %collective-permute-start.14 = (bf16[2,4,2,16,16,128]{5,4,3,2,1,0:T(8,128)(2,1)}, bf16[2,4,2,16,16,128]{5,4,3,2,1,0:T(8,128)(2,1)S(1)}, u32[]{:S(2)}, u32[]{:S(2)}) collective-permute-start(bf16[2,4,2,16,16,128]{5,4,3,2,1,0:T(8,128)(2,1)} %bitcast.35), channel_id=1, source_target_pairs={{0,96},{1,33},{2,98},{3,35},{4,100},{5,37},{6,102},{7,39},{8,104},... | collective-permute-start | bytes 3145736 | tf_op jit(solution)/shard_map/ppermute | solution.py:713
  186.3 15.9 %att_bwd.2 = (bf16[528,512]{1,0:T(8,128)(2,1)S(1)}, bf16[528,1024]{1,0:T(8,128)(2,1)S(1)}, bf16[512,1024]{1,0:T(8,128)(2,1)S(1)}) custom-call(bf16[528,1024]{1,0:T(8,128)(2,1)S(1)} %copy-done.8, bf16[528,1024]{1,0:T(8,128)(2,1)S(1)} %copy-done.21, bf16[528,1024]{1,0:T(8,128)(2,1)S(1)} %copy-done.21, bf16[528,1024]{1,0:T(8,128)(2,1)S(1)} %copy-done.24, ...), custom_call_target="tpu_custom_call" | custom-call | flops 5536481280 | bytes 8650752 | tf_op jit(solution)/shard_map/att_bwd/pallas_call | solution.py:194
  202.8 1.5 far_sum.5
  207.5 1.9 near_sum.10
  209.4 2.1 collective-permute-start.17
  211.5 16.7 %att_bwd.3 = (bf16[528,512]{1,0:T(8,128)(2,1)S(1)}, bf16[528,1024]{1,0:T(8,128)(2,1)S(1)}, bf16[512,1024]{1,0:T(8,128)(2,1)}) custom-call(bf16[528,1024]{1,0:T(8,128)(2,1)S(1)} %copy-done.8, bf16[528,1024]{1,0:T(8,128)(2,1)S(1)} %copy-done.6, bf16[528,1024]{1,0:T(8,128)(2,1)S(1)} %copy-done.6, bf16[528,1024]{1,0:T(8,128)(2,1)S(1)} %copy-done.18, ...), custom_call_target="tpu_custom_call" | custom-call | flops 5536481280 | bytes 8650752 | tf_op jit(solution)/shard_map/att_bwd/pallas_call | solution.py:194
  230.7 1.4 near_sum.11
  233.8 8.6 %dw_near.4 = (bf16[2,2,4,2,10,16,128]{6,5,4,3,2,1,0:T(8,128)(2,1)}, bf16[2,2,4,2,10,16,128]{6,5,4,3,2,1,0:T(8,128)(2,1)}) custom-call(s32[10]{0:T(128)S(1)} %copy-done.14, bf16[528,1024]{1,0:T(8,128)(2,1)S(1)} %copy-done.28, bf16[528,1024]{1,0:T(8,128)(2,1)S(1)} %copy-done.26, bf16[528,512]{1,0:T(8,128)(2,1)S(1)} %constant_dynamic-slice_fusion.1.refs_2_, ...), custom_call_target="tpu_custom_call" | custom-call | flops 2768240640 | bytes 9650176 | tf_op jit(solution)/shard_map/dw_near/pallas_call | solution.py:439
  242.4 1.1 trip.3
  244.8 9.9 %tok_bwd.1 = (f32[256,1024]{1,0:T(8,128)S(1)}, bf16[272,1024]{1,0:T(8,128)(2,1)S(1)}, bf16[1024,512]{1,0:T(8,128)(2,1)S(1)}, f32[8,1024]{1,0:T(8,128)S(1)}, f32[...) custom-call(s32[10]{0:T(128)S(1)} %copy-done.14, bf16[528,768]{1,0:T(8,128)(2,1)S(1)} %get-tuple-element.155.refs_6_.g_mine0, ...), custom_call_target="tpu_custom_call" | custom-call | flops 3321888768 | bytes 14942208 | tf_op jit(solution)/shard_map/tok_bwd/pallas_call | solution.py:529
  254.8 9.4 %dw_near.5 = (bf16[2,2,4,2,11,16,128]{6,5,4,3,2,1,0:T(8,128)(2,1)}, bf16[2,2,4,2,11,16,128]{6,5,4,3,2,1,0:T(8,128)(2,1)}) custom-call(s32[10]{0:T(128)S(1)} %copy-done.14, bf16[528,1024]{1,0:T(8,128)(2,1)S(1)} %get-tuple-element.195.x_ref.refs_4_.refs_0_, bf16[528,1024]{1,0:T(8,128)(2,1)} %collective-permute-done.19.refs_5_.refs_1_, ...), custom_call_target="tpu_custom_call" | custom-call | flops 1660944384 | bytes 7864320 | tf_op jit(solution)/shard_map/dw_near/pallas_call | solution.py:439
  264.2 1.9 collective-permute-start.30
  266.2 17.2 %collective-permute-done.30 = bf16[2,2,4,2,11,16,128]{6,5,4,3,2,1,0:T(8,128)(2,1)S(1)} collective-permute-done((bf16[2,2,4,2,11,16,128]{6,5,4,3,2,1,0:T(8,128)(2,1)}, bf16[2,2,4,2,11,16,128]{6,5,4,3,2,1,0:T(8,128)(2,1)S(1)}, u32[]{:S(2)}, u32[]{:S(2)}) %collective-permute-start.30) | collective-permute-done | bytes 1441824 | tf_op jit(solution)/shard_map/ppermute | solution.py:713
  283.4 1.4 copy-done.3
  285.3 4.1 %collective-permute-start.31 = (bf16[2,4,2,11,16,128]{5,4,3,2,1,0:T(8,128)(2,1)S(1)}, bf16[2,4,2,11,16,128]{5,4,3,2,1,0:T(8,128)(2,1)S(1)}, u32[]{:S(2)}, u32[]{:S(2)}) collective-permute-start(bf16[2,4,2,11,16,128]{5,4,3,2,1,0:T(8,128)(2,1)S(1)} %bitcast.137), channel_id=1, source_target_pairs={{0,96},{1,33},{2,98},{3,35},{4,100},{5,37},{6,102},{7,39},{8,104},... | collective-permute-start | bytes 2162696 | tf_op jit(solution)/shard_map/ppermute | solution.py:713
  289.5 15.7 %collective-permute-done.25 = bf16[2,2,4,2,10,16,128]{6,5,4,3,2,1,0:T(8,128)(2,1)S(1)} collective-permute-done((bf16[2,2,4,2,10,16,128]{6,5,4,3,2,1,0:T(8,128)(2,1)S(1)}, bf16[2,2,4,2,10,16,128]{6,5,4,3,2,1,0:T(8,128)(2,1)S(1)}, u32[]{:S(2)}, u32[]{:S(2)}) %collective-permute-start.25) | collective-permute-done | bytes 1310752 | tf_op jit(solution)/shard_map/ppermute | solution.py:713
  305.7 4.1 %collective-permute-start.26 = (bf16[2,4,2,10,16,128]{5,4,3,2,1,0:T(8,128)(2,1)S(1)}, bf16[2,4,2,10,16,128]{5,4,3,2,1,0:T(8,128)(2,1)S(1)}, u32[]{:S(2)}, u32[]{:S(2)}) collective-permute-start(bf16[2,4,2,10,16,128]{5,4,3,2,1,0:T(8,128)(2,1)S(1)} %bitcast.138), channel_id=1, source_target_pairs={{0,96},{1,33},{2,98},{3,35},{4,100},{5,37},{6,102},{7,39},{8,104},... | collective-permute-start | bytes 1966088 | tf_op jit(solution)/shard_map/ppermute | solution.py:713
  310.7 2.0 collective-permute-start.5
  312.7 1.4 far_sum.8
  314.3 9.7 %collective-permute-done.26.refs_1_ = bf16[2,4,2,10,16,128]{5,4,3,2,1,0:T(8,128)(2,1)S(1)} collective-permute-done((bf16[2,4,2,10,16,128]{5,4,3,2,1,0:T(8,128)(2,1)S(1)}, bf16[2,4,2,10,16,128]{5,4,3,2,1,0:T(8,128)(2,1)S(1)}, u32[]{:S(2)}, u32[]{:S(2)}) %collective-permute-start.26) | collective-permute-done | bytes 655392 | tf_op jit(solution)/shard_map/ppermute | solution.py:713
  324.0 1.4 far_sum.7
  325.6 1.7 collective-permute-start.22
  327.3 1.4 near_sum.12
  328.8 3.0 collective-permute-start.24
  332.8 2.0 collective-permute-start.21
  334.8 1.9 near_sum.14
  336.7 1.9 collective-permute-start.28
  338.6 1.9 near_sum.16
  340.6 1.5 collective-permute-start.33
  343.9 3.5 collective-permute-done.33.refs_7_
  347.4 2.5 far_sum.9
  351.8 2.0 copy.44
  355.3 1.2 convert_element_type.49
  356.4 4.1 %collective-permute-done.34.came_ref = bf16[2,53,16,128]{3,2,1,0:T(8,128)(2,1)S(1)} collective-permute-done((bf16[2,53,16,128]{3,2,1,0:T(8,128)(2,1)}, bf16[2,53,16,128]{3,2,1,0:T(8,128)(2,1)S(1)}, u32[]{:S(2)}, u32[]{:S(2)}) %collective-permute-start.34) | collective-permute-done | bytes 434208 | tf_op jit(solution)/shard_map/ppermute | solution.py:713
  360.7 2.3 collective-permute-start.35
  363.1 4.8 %collective-permute-done.35.came_ref = bf16[53,16,128]{2,1,0:T(8,128)(2,1)S(1)} collective-permute-done((bf16[53,16,128]{2,1,0:T(8,128)(2,1)S(1)}, bf16[53,16,128]{2,1,0:T(8,128)(2,1)S(1)}, u32[]{:S(2)}, u32[]{:S(2)}) %collective-permute-start.35) | collective-permute-done | bytes 217120 | tf_op jit(solution)/shard_map/ppermute | solution.py:713
  367.9 1.2 last_sum.1
  369.3 2.9 copy.45
  372.3 1.3 finish.1
  (193 shorter events, 32.7 us)
Async XLA Ops:
  1.4 5.2 %copy-start.39 = (bf16[256,1024]{1,0:T(8,128)(2,1)S(1)}, bf16[256,1024]{1,0:T(8,128)(2,1)}, u32[]{:S(2)}) copy-start(bf16[256,1024]{1,0:T(8,128)(2,1)} %param.25) | copy-start | bytes 1572868
  1.4 7.4 %copy-start.44 = (f32[2048]{0:T(1024)S(1)}, f32[2048]{0:T(1024)}, u32[]{:S(2)}) copy-start(f32[2048]{0:T(1024)} %param.29) | copy-start | bytes 24580
  1.4 7.5 %copy-start.42 = (bf16[2,1024]{1,0:T(2,128)(2,1)S(1)}, bf16[2,1024]{1,0:T(2,128)(2,1)}, u32[]{:S(2)}) copy-start(bf16[2,1024]{1,0:T(2,128)(2,1)} %param.22) | copy-start | bytes 12292
  1.4 20.2 %slice-start = ((s8[6291456]{0:T(1024)(128)(4,1)}), s8[4194304]{0:T(1024)(128)(4,1)S(1)}, s32[]{:S(2)}) async-start(s8[6291456]{0:T(1024)(128)(4,1)} %bitcast.107), calls=%async_computation | async-start | bytes 8388608
  4.8 13.7 %collective-permute-start = (bf16[256,1024]{1,0:T(8,128)(2,1)S(1)}, bf16[256,1024]{1,0:T(8,128)(2,1)S(1)}, u32[]{:S(2)}, u32[]{:S(2)}) collective-permute-start(bf16[256,1024]{1,0:T(8,128)(2,1)S(1)} %select_bitcast_fusion.2), channel_id=1, source_target_pairs={{0,2},{2,0},{1,3},{3,1},{4,6},{6,4},{5,7},{7,5},{8,10},{10,8},{9,1... | collective-permute-start | bytes 1572872 | tf_op jit(solution)/shard_map/ppermute | solution.py:694
  6.5 14.6 %collective-permute-start.1 = (bf16[256,1024]{1,0:T(8,128)(2,1)S(1)}, bf16[256,1024]{1,0:T(8,128)(2,1)S(1)}, u32[]{:S(2)}, u32[]{:S(2)}) collective-permute-start(bf16[256,1024]{1,0:T(8,128)(2,1)S(1)} %copy-done.39), channel_id=1, source_target_pairs={{0,18},{18,0},{2,16},{16,2},{1,19},{19,1},{3,17},{17,3},{4,22},{22... | collective-permute-start | bytes 1572872 | tf_op jit(solution)/shard_map/ppermute | solution.py:760
  8.8 12.7 %slice-start.1 = ((s8[6291456]{0:T(1024)(128)(4,1)}), s8[2097152]{0:T(1024)(128)(4,1)S(1)}, s32[]{:S(2)}) async-start(s8[6291456]{0:T(1024)(128)(4,1)} %bitcast.107), calls=%async_computation.1 | async-start | bytes 4194304
  24.4 2.8 collective-permute-start.2
  26.3 21.6 %copy-start.5 = (bf16[528,1024]{1,0:T(8,128)(2,1)}, bf16[528,1024]{1,0:T(8,128)(2,1)S(1)}, u32[]{:S(2)}) copy-start(bf16[528,1024]{1,0:T(8,128)(2,1)S(1)} %project.2.ko_ref.vo_ref) | copy-start | bytes 3244036
  26.3 5.5 %copy-start.43 = (bf16[2,1024]{1,0:T(2,128)(2,1)S(1)}, bf16[2,1024]{1,0:T(2,128)(2,1)}, u32[]{:S(2)}) copy-start(bf16[2,1024]{1,0:T(2,128)(2,1)} %param.41) | copy-start | bytes 12292
  28.3 19.6 %collective-permute-start.3 = (bf16[528,1024]{1,0:T(8,128)(2,1)S(1)}, bf16[528,1024]{1,0:T(8,128)(2,1)S(1)}, u32[]{:S(2)}, u32[]{:S(2)}) collective-permute-start(bf16[528,1024]{1,0:T(8,128)(2,1)S(1)} %project.2.ko_ref.vo_ref), channel_id=1, source_target_pairs={{0,1},{1,0},{2,3},{3,2},{4,5},{5,4},{6,7},{7,6},{8,9},{9,8},{10,11... | collective-permute-start | bytes 3244040 | tf_op jit(solution)/shard_map/ppermute | solution.py:694
  31.5 27.2 %collective-permute-start.4 = (bf16[256,1152]{1,0:T(8,128)(2,1)}, bf16[256,1152]{1,0:T(8,128)(2,1)}, u32[]{:S(2)}, u32[]{:S(2)}) collective-permute-start(bf16[256,1152]{1,0:T(8,128)(2,1)} %pad_maximum_fusion), channel_id=1, source_target_pairs={{0,2},{2,0},{1,3},{3,1},{4,6},{6,4},{5,7},{7,5},{8,10},{10,8},{9,1... | collective-permute-start | bytes 1769480 | tf_op jit(solution)/shard_map/ppermute | solution.py:694
  37.1 10.8 %copy-start.7 = (bf16[528,1024]{1,0:T(8,128)(2,1)}, bf16[528,1024]{1,0:T(8,128)(2,1)S(1)}, u32[]{:S(2)}) copy-start(bf16[528,1024]{1,0:T(8,128)(2,1)S(1)} %project.3.q_ref) | copy-start | bytes 3244036
  47.8 10.8 %copy-start.33 = (f32[528,512]{1,0:T(8,128)}, f32[528,512]{1,0:T(8,128)S(1)}, u32[]{:S(2)}) copy-start(f32[528,512]{1,0:T(8,128)S(1)} %get-tuple-element.151.lse_ref) | copy-start | bytes 3244036
  47.9 10.8 %copy-start.17 = (bf16[528,1024]{1,0:T(8,128)(2,1)}, bf16[528,1024]{1,0:T(8,128)(2,1)S(1)}, u32[]{:S(2)}) copy-start(bf16[528,1024]{1,0:T(8,128)(2,1)S(1)} %collective-permute-done.3.kp_ref.vp_ref) | copy-start | bytes 3244036
  47.9 12.3 %copy-start.37 = (bf16[256,1024]{1,0:T(8,128)(2,1)S(1)}, bf16[256,1024]{1,0:T(8,128)(2,1)}, u32[]{:S(2)}) copy-start(bf16[256,1024]{1,0:T(8,128)(2,1)} %get-tuple-element.245) | copy-start | bytes 1572868
  61.4 37.5 %copy-start.13 = (s32[10]{0:T(128)S(1)}, s32[10]{0:T(128)}, u32[]{:S(2)}) copy-start(s32[10]{0:T(128)} %stack.141.order_ref) | copy-start | bytes 124
  87.3 2.2 collective-permute-start.6
  90.3 7.7 %collective-permute-start.7 = (bf16[528,4096]{1,0:T(8,128)(2,1)}, bf16[528,4096]{1,0:T(8,128)(2,1)}, u32[]{:S(2)}, u32[]{:S(2)}) collective-permute-start(bf16[528,4096]{1,0:T(8,128)(2,1)} %get-tuple-element.134.refs_0_), channel_id=1, source_target_pairs={{0,1},{1,0},{2,3},{3,2},{4,5},{5,4},{6,7},{7,6},{8,9},{9,8},{10,11... | collective-permute-start | bytes 12976136 | tf_op jit(solution)/shard_map/ppermute | solution.py:694
  98.0 41.1 %collective-permute-start.9 = (bf16[528,1024]{1,0:T(8,128)(2,1)}, bf16[528,1024]{1,0:T(8,128)(2,1)S(1)}, u32[]{:S(2)}, u32[]{:S(2)}) collective-permute-start(bf16[528,1024]{1,0:T(8,128)(2,1)} %copy-done.27), channel_id=1, source_target_pairs={{0,1},{1,0},{2,3},{3,2},{4,5},{5,4},{6,7},{7,6},{8,9},{9,8},{10,11... | collective-permute-start | bytes 3244040 | tf_op jit(solution)/shard_map/ppermute | solution.py:694
  137.0 30.3 %collective-permute-start.11 = (bf16[528,2048]{1,0:T(8,128)(2,1)}, bf16[528,2048]{1,0:T(8,128)(2,1)}, u32[]{:S(2)}, u32[]{:S(2)}) collective-permute-start(bf16[528,2048]{1,0:T(8,128)(2,1)} %get-tuple-element.148), channel_id=1, source_target_pairs={{0,1},{1,0},{2,3},{3,2},{4,5},{5,4},{6,7},{7,6},{8,9},{9,8},{10,11... | collective-permute-start | bytes 6488072 | tf_op jit(solution)/shard_map/ppermute | solution.py:694
  137.2 26.4 %collective-permute-start.8 = (bf16[2,2,4,2,16,16,128]{6,5,4,3,2,1,0:T(8,128)(2,1)}, bf16[2,2,4,2,16,16,128]{6,5,4,3,2,1,0:T(8,128)(2,1)}, u32[]{:S(2)}, u32[]{:S(2)}) collective-permute-start(bf16[2,2,4,2,16,16,128]{6,5,4,3,2,1,0:T(8,128)(2,1)} %get-tuple-element.135), channel_id=1, source_target_pairs={{0,32},{1,97},{2,34},{3,99},{4,36},{5,101},{6,38},{7,103},{8,40},{... | collective-permute-start | bytes 6291464 | tf_op jit(solution)/shard_map/ppermute | solution.py:713
  140.2 27.2 %collective-permute-start.10 = (bf16[528,1024]{1,0:T(8,128)(2,1)}, bf16[528,1024]{1,0:T(8,128)(2,1)}, u32[]{:S(2)}, u32[]{:S(2)}) collective-permute-start(bf16[528,1024]{1,0:T(8,128)(2,1)} %get-tuple-element.146.a0_ref), channel_id=1, source_target_pairs={{0,1},{1,0},{2,3},{3,2},{4,5},{5,4},{6,7},{7,6},{8,9},{9,8},{10,11... | collective-permute-start | bytes 3244040 | tf_op jit(solution)/shard_map/ppermute | solution.py:694
  167.3 18.9 %copy-start.8 = (bf16[528,1024]{1,0:T(8,128)(2,1)S(1)}, bf16[528,1024]{1,0:T(8,128)(2,1)}, u32[]{:S(2)}) copy-start(bf16[528,1024]{1,0:T(8,128)(2,1)} %copy-done.7) | copy-start | bytes 3244036
  167.3 18.9 %copy-start.21 = (bf16[528,1024]{1,0:T(8,128)(2,1)S(1)}, bf16[528,1024]{1,0:T(8,128)(2,1)}, u32[]{:S(2)}) copy-start(bf16[528,1024]{1,0:T(8,128)(2,1)} %copy-done.19) | copy-start | bytes 3244036
  167.3 18.9 %copy-start.24 = (bf16[528,1024]{1,0:T(8,128)(2,1)S(1)}, bf16[528,1024]{1,0:T(8,128)(2,1)}, u32[]{:S(2)}) copy-start(bf16[528,1024]{1,0:T(8,128)(2,1)} %copy-done.22) | copy-start | bytes 3244036
  180.6 26.9 %collective-permute-start.13 = (bf16[2,4,2,2,16,16,128]{6,5,4,3,2,1,0:T(8,128)(2,1)}, bf16[2,4,2,2,16,16,128]{6,5,4,3,2,1,0:T(8,128)(2,1)S(1)}, u32[]{:S(2)}, u32[]{:S(2)}) collective-permute-start(bf16[2,4,2,2,16,16,128]{6,5,4,3,2,1,0:T(8,128)(2,1)} %get-tuple-element.149), channel_id=1, source_target_pairs={{0,4},{1,13},{2,6},{3,15},{4,0},{5,9},{6,2},{7,11},{8,12},{9,5},{1... | collective-permute-start | bytes 6291464 | tf_op jit(solution)/shard_map/ppermute | solution.py:713
  182.1 20.8 %collective-permute-start.14 = (bf16[2,4,2,16,16,128]{5,4,3,2,1,0:T(8,128)(2,1)}, bf16[2,4,2,16,16,128]{5,4,3,2,1,0:T(8,128)(2,1)S(1)}, u32[]{:S(2)}, u32[]{:S(2)}) collective-permute-start(bf16[2,4,2,16,16,128]{5,4,3,2,1,0:T(8,128)(2,1)} %bitcast.35), channel_id=1, source_target_pairs={{0,96},{1,33},{2,98},{3,35},{4,100},{5,37},{6,102},{7,39},{8,104},... | collective-permute-start | bytes 3145736 | tf_op jit(solution)/shard_map/ppermute | solution.py:713
  202.2 3.3 copy-start.14
  202.2 3.3 collective-permute-start.12
  202.3 31.4 %collective-permute-start.19 = (bf16[528,1024]{1,0:T(8,128)(2,1)S(1)}, bf16[528,1024]{1,0:T(8,128)(2,1)}, u32[]{:S(2)}, u32[]{:S(2)}) collective-permute-start(bf16[528,1024]{1,0:T(8,128)(2,1)S(1)} %get-tuple-element.195.x_ref.refs_4_.refs_0_), channel_id=1, source_target_pairs={{0,1},{1,0},{2,3},{3,2},{4,5},{5,4},{6,7},{7,6},{8,9},{9,8},{10,11... | collective-permute-start | bytes 3244040 | tf_op jit(solution)/shard_map/ppermute | solution.py:694
  204.3 23.8 %collective-permute-start.18 = (bf16[2,2,2,16,16,128]{5,4,3,2,1,0:T(8,128)(2,1)}, bf16[2,2,2,16,16,128]{5,4,3,2,1,0:T(8,128)(2,1)S(1)}, u32[]{:S(2)}, u32[]{:S(2)}) collective-permute-start(bf16[2,2,2,16,16,128]{5,4,3,2,1,0:T(8,128)(2,1)} %get-tuple-element.160), channel_id=1, source_target_pairs={{0,4},{1,13},{2,6},{3,15},{4,0},{5,9},{6,2},{7,11},{8,12},{9,5},{1... | collective-permute-start | bytes 1572872 | tf_op jit(solution)/shard_map/ppermute | solution.py:713
  206.7 27.1 %collective-permute-start.20 = (bf16[528,768]{1,0:T(8,128)(2,1)S(1)}, bf16[528,768]{1,0:T(8,128)(2,1)}, u32[]{:S(2)}, u32[]{:S(2)}) collective-permute-start(bf16[528,768]{1,0:T(8,128)(2,1)S(1)} %get-tuple-element.156.g_send0), channel_id=1, source_target_pairs={{0,1},{1,0},{2,3},{3,2},{4,5},{5,4},{6,7},{7,6},{8,9},{9,8},{10,11... | collective-permute-start | bytes 2433032 | tf_op jit(solution)/shard_map/ppermute | solution.py:694
  207.5 4.0 %copy-start.6 = (bf16[528,1024]{1,0:T(8,128)(2,1)S(1)}, bf16[528,1024]{1,0:T(8,128)(2,1)}, u32[]{:S(2)}) copy-start(bf16[528,1024]{1,0:T(8,128)(2,1)} %copy-done.5) | copy-start | bytes 3244036
  207.5 4.0 %copy-start.18 = (bf16[528,1024]{1,0:T(8,128)(2,1)S(1)}, bf16[528,1024]{1,0:T(8,128)(2,1)}, u32[]{:S(2)}) copy-start(bf16[528,1024]{1,0:T(8,128)(2,1)} %copy-done.17) | copy-start | bytes 3244036
  209.4 23.6 %collective-permute-start.17 = (bf16[4,2,2,16,16,128]{5,4,3,2,1,0:T(8,128)(2,1)}, bf16[4,2,2,16,16,128]{5,4,3,2,1,0:T(8,128)(2,1)S(1)}, u32[]{:S(2)}, u32[]{:S(2)}) collective-permute-start(bf16[4,2,2,16,16,128]{5,4,3,2,1,0:T(8,128)(2,1)} %bitcast.38), channel_id=1, source_target_pairs={{0,12},{1,5},{2,14},{3,7},{4,8},{5,1},{6,10},{7,3},{8,4},{9,13},{1... | collective-permute-start | bytes 3145736 | tf_op jit(solution)/shard_map/ppermute | solution.py:713
  211.5 18.2 %copy-start.40 = (bf16[528,1024]{1,0:T(8,128)(2,1)S(1)}, bf16[528,1024]{1,0:T(8,128)(2,1)}, u32[]{:S(2)}) copy-start(bf16[528,1024]{1,0:T(8,128)(2,1)} %get-tuple-element.166) | copy-start | bytes 3244036
  228.1 14.3 %collective-permute-start.15 = (bf16[512,1024]{1,0:T(8,128)(2,1)}, bf16[512,1024]{1,0:T(8,128)(2,1)S(1)}, u32[]{:S(2)}, u32[]{:S(2)}) collective-permute-start(bf16[512,1024]{1,0:T(8,128)(2,1)} %get-tuple-element.165), channel_id=1, source_target_pairs={{0,1},{1,0},{2,3},{3,2},{4,5},{5,4},{6,7},{7,6},{8,9},{9,8},{10,11... | collective-permute-start | bytes 3145736 | tf_op jit(solution)/shard_map/ppermute | solution.py:694
  229.0 4.8 %collective-permute-start.16 = (bf16[528,512]{1,0:T(8,128)(2,1)}, bf16[528,512]{1,0:T(8,128)(2,1)S(1)}, u32[]{:S(2)}, u32[]{:S(2)}) collective-permute-start(bf16[528,512]{1,0:T(8,128)(2,1)} %get-tuple-element.168), channel_id=1, source_target_pairs={{0,1},{1,0},{2,3},{3,2},{4,5},{5,4},{6,7},{7,6},{8,9},{9,8},{10,11... | collective-permute-start | bytes 1622024 | tf_op jit(solution)/shard_map/ppermute | solution.py:694
  243.5 11.2 %collective-permute-start.29 = (bf16[528,768]{1,0:T(8,128)(2,1)S(1)}, bf16[528,768]{1,0:T(8,128)(2,1)S(1)}, u32[]{:S(2)}, u32[]{:S(2)}) collective-permute-start(bf16[528,768]{1,0:T(8,128)(2,1)S(1)} %get-tuple-element.178.g_send1), channel_id=1, source_target_pairs={{0,1},{1,0},{2,3},{3,2},{4,5},{5,4},{6,7},{7,6},{8,9},{9,8},{10,11... | collective-permute-start | bytes 2433032 | tf_op jit(solution)/shard_map/ppermute | solution.py:694
  244.7 10.0 %copy-start.34 = (f32[8,4096]{1,0:T(8,128)S(1)}, f32[8,4096]{1,0:T(8,128)}, u32[]{:S(2)}) copy-start(f32[8,4096]{1,0:T(8,128)} %get-tuple-element.199.refs_8_) | copy-start | bytes 393220
  244.7 10.0 %copy-start.35 = (f32[8,1024]{1,0:T(8,128)S(1)}, f32[8,1024]{1,0:T(8,128)}, u32[]{:S(2)}) copy-start(f32[8,1024]{1,0:T(8,128)} %get-tuple-element.196.refs_5_) | copy-start | bytes 98308
  244.7 10.0 %copy-start.36 = (f32[8,1024]{1,0:T(8,128)S(1)}, f32[8,1024]{1,0:T(8,128)}, u32[]{:S(2)}) copy-start(f32[8,1024]{1,0:T(8,128)} %get-tuple-element.197.refs_6_) | copy-start | bytes 98308
  254.7 56.0 %copy-start.29 = (bf16[272,1024]{1,0:T(8,128)(2,1)}, bf16[272,1024]{1,0:T(8,128)(2,1)S(1)}, u32[]{:S(2)}) copy-start(bf16[272,1024]{1,0:T(8,128)(2,1)S(1)} %get-tuple-element.180) | copy-start | bytes 1671172
  254.8 11.3 %copy-start.45 = (bf16[2,2,4,2,10,16,128]{6,5,4,3,2,1,0:T(8,128)(2,1)S(1)}, bf16[2,2,4,2,10,16,128]{6,5,4,3,2,1,0:T(8,128)(2,1)}, u32[]{:S(2)}) copy-start(bf16[2,2,4,2,10,16,128]{6,5,4,3,2,1,0:T(8,128)(2,1)} %get-tuple-element.175) | copy-start | bytes 3932164
  254.8 50.4 %copy-start.4 = (bf16[2,2,4,2,10,16,128]{6,5,4,3,2,1,0:T(8,128)(2,1)S(1)}, bf16[2,2,4,2,10,16,128]{6,5,4,3,2,1,0:T(8,128)(2,1)}, u32[]{:S(2)}) copy-start(bf16[2,2,4,2,10,16,128]{6,5,4,3,2,1,0:T(8,128)(2,1)} %get-tuple-element.187) | copy-start | bytes 3932164
  264.2 19.2 %collective-permute-start.30 = (bf16[2,2,4,2,11,16,128]{6,5,4,3,2,1,0:T(8,128)(2,1)}, bf16[2,2,4,2,11,16,128]{6,5,4,3,2,1,0:T(8,128)(2,1)S(1)}, u32[]{:S(2)}, u32[]{:S(2)}) collective-permute-start(bf16[2,2,4,2,11,16,128]{6,5,4,3,2,1,0:T(8,128)(2,1)} %get-tuple-element.202), channel_id=1, source_target_pairs={{0,32},{1,97},{2,34},{3,99},{4,36},{5,101},{6,38},{7,103},{8,40},{... | collective-permute-start | bytes 4325384 | tf_op jit(solution)/shard_map/ppermute | solution.py:713
  266.1 39.1 %collective-permute-start.25 = (bf16[2,2,4,2,10,16,128]{6,5,4,3,2,1,0:T(8,128)(2,1)S(1)}, bf16[2,2,4,2,10,16,128]{6,5,4,3,2,1,0:T(8,128)(2,1)S(1)}, u32[]{:S(2)}, u32[]{:S(2)}) collective-permute-start(bf16[2,2,4,2,10,16,128]{6,5,4,3,2,1,0:T(8,128)(2,1)S(1)} %copy-done.45), channel_id=1, source_target_pairs={{0,32},{1,97},{2,34},{3,99},{4,36},{5,101},{6,38},{7,103},{8,40},{... | collective-permute-start | bytes 3932168 | tf_op jit(solution)/shard_map/ppermute | solution.py:713
  284.7 25.1 %copy-start.38 = (bf16[528,1024]{1,0:T(8,128)(2,1)S(1)}, bf16[528,1024]{1,0:T(8,128)(2,1)}, u32[]{:S(2)}) copy-start(bf16[528,1024]{1,0:T(8,128)(2,1)} %get-tuple-element.130) | copy-start | bytes 3244036
  285.3 27.3 %collective-permute-start.31 = (bf16[2,4,2,11,16,128]{5,4,3,2,1,0:T(8,128)(2,1)S(1)}, bf16[2,4,2,11,16,128]{5,4,3,2,1,0:T(8,128)(2,1)S(1)}, u32[]{:S(2)}, u32[]{:S(2)}) collective-permute-start(bf16[2,4,2,11,16,128]{5,4,3,2,1,0:T(8,128)(2,1)S(1)} %bitcast.137), channel_id=1, source_target_pairs={{0,96},{1,33},{2,98},{3,35},{4,100},{5,37},{6,102},{7,39},{8,104},... | collective-permute-start | bytes 2162696 | tf_op jit(solution)/shard_map/ppermute | solution.py:713
  305.7 18.3 %collective-permute-start.26 = (bf16[2,4,2,10,16,128]{5,4,3,2,1,0:T(8,128)(2,1)S(1)}, bf16[2,4,2,10,16,128]{5,4,3,2,1,0:T(8,128)(2,1)S(1)}, u32[]{:S(2)}, u32[]{:S(2)}) collective-permute-start(bf16[2,4,2,10,16,128]{5,4,3,2,1,0:T(8,128)(2,1)S(1)} %bitcast.138), channel_id=1, source_target_pairs={{0,96},{1,33},{2,98},{3,35},{4,100},{5,37},{6,102},{7,39},{8,104},... | collective-permute-start | bytes 1966088 | tf_op jit(solution)/shard_map/ppermute | solution.py:713
  309.8 17.5 %collective-permute-start.23 = (bf16[2,2,2,16,16,128]{5,4,3,2,1,0:T(8,128)(2,1)S(1)}, bf16[2,2,2,16,16,128]{5,4,3,2,1,0:T(8,128)(2,1)S(1)}, u32[]{:S(2)}, u32[]{:S(2)}) collective-permute-start(bf16[2,2,2,16,16,128]{5,4,3,2,1,0:T(8,128)(2,1)S(1)} %get-tuple-element.170), channel_id=1, source_target_pairs={{0,32},{1,97},{2,34},{3,99},{4,36},{5,101},{6,38},{7,103},{8,40},{... | collective-permute-start | bytes 1572872 | tf_op jit(solution)/shard_map/ppermute | solution.py:713
  310.7 29.9 %collective-permute-start.5 = (bf16[272,1024]{1,0:T(8,128)(2,1)}, bf16[272,1024]{1,0:T(8,128)(2,1)}, u32[]{:S(2)}, u32[]{:S(2)}) collective-permute-start(bf16[272,1024]{1,0:T(8,128)(2,1)} %slice.152), channel_id=1, source_target_pairs={{0,2},{2,0},{1,3},{3,1},{4,6},{6,4},{5,7},{7,5},{8,10},{10,8},{9,1... | collective-permute-start | bytes 1671176 | tf_op jit(solution)/shard_map/ppermute | solution.py:694
  314.1 22.6 %collective-permute-start.32 = (bf16[2,2,2,11,16,128]{5,4,3,2,1,0:T(8,128)(2,1)}, bf16[2,2,2,11,16,128]{5,4,3,2,1,0:T(8,128)(2,1)}, u32[]{:S(2)}, u32[]{:S(2)}) collective-permute-start(bf16[2,2,2,11,16,128]{5,4,3,2,1,0:T(8,128)(2,1)} %get-tuple-element.206), channel_id=1, source_target_pairs={{0,4},{1,13},{2,6},{3,15},{4,0},{5,9},{6,2},{7,11},{8,12},{9,5},{1... | collective-permute-start | bytes 1081352 | tf_op jit(solution)/shard_map/ppermute | solution.py:713
  325.4 7.4 %collective-permute-start.27 = (bf16[2,2,2,10,16,128]{5,4,3,2,1,0:T(8,128)(2,1)}, bf16[2,2,2,10,16,128]{5,4,3,2,1,0:T(8,128)(2,1)}, u32[]{:S(2)}, u32[]{:S(2)}) collective-permute-start(bf16[2,2,2,10,16,128]{5,4,3,2,1,0:T(8,128)(2,1)} %get-tuple-element.191), channel_id=1, source_target_pairs={{0,4},{1,13},{2,6},{3,15},{4,0},{5,9},{6,2},{7,11},{8,12},{9,5},{1... | collective-permute-start | bytes 983048 | tf_op jit(solution)/shard_map/ppermute | solution.py:713
  325.6 18.3 %collective-permute-start.22 = (bf16[2,2,16,16,128]{4,3,2,1,0:T(8,128)(2,1)}, bf16[2,2,16,16,128]{4,3,2,1,0:T(8,128)(2,1)}, u32[]{:S(2)}, u32[]{:S(2)}) collective-permute-start(bf16[2,2,16,16,128]{4,3,2,1,0:T(8,128)(2,1)} %bitcast.43), channel_id=1, source_target_pairs={{0,12},{1,5},{2,14},{3,7},{4,8},{5,1},{6,10},{7,3},{8,4},{9,13},{1... | collective-permute-start | bytes 786440 | tf_op jit(solution)/shard_map/ppermute | solution.py:713
  327.3 20.1 %copy-start.12 = (f32[64,16,128]{2,1,0:T(8,128)S(1)}, f32[64,16,128]{2,1,0:T(8,128)}, u32[]{:S(2)}) copy-start(f32[64,16,128]{2,1,0:T(8,128)} %copy-done.11) | copy-start | bytes 1572868
  328.8 15.1 %collective-permute-start.24 = (bf16[2,2,16,16,128]{4,3,2,1,0:T(8,128)(2,1)}, bf16[2,2,16,16,128]{4,3,2,1,0:T(8,128)(2,1)}, u32[]{:S(2)}, u32[]{:S(2)}) collective-permute-start(bf16[2,2,16,16,128]{4,3,2,1,0:T(8,128)(2,1)} %bitcast.59), channel_id=1, source_target_pairs={{0,96},{1,33},{2,98},{3,35},{4,100},{5,37},{6,102},{7,39},{8,104},... | collective-permute-start | bytes 786440 | tf_op jit(solution)/shard_map/ppermute | solution.py:713
  332.8 21.8 %collective-permute-start.21 = (bf16[272,1024]{1,0:T(8,128)(2,1)}, bf16[272,1024]{1,0:T(8,128)(2,1)}, u32[]{:S(2)}, u32[]{:S(2)}) collective-permute-start(bf16[272,1024]{1,0:T(8,128)(2,1)} %copy-done.29), channel_id=1, source_target_pairs={{0,2},{2,0},{1,3},{3,1},{4,6},{6,4},{5,7},{7,5},{8,10},{10,8},{9,1... | collective-permute-start | bytes 1671176 | tf_op jit(solution)/shard_map/ppermute | solution.py:694
  336.7 7.2 %collective-permute-start.28 = (bf16[2,2,10,16,128]{4,3,2,1,0:T(8,128)(2,1)S(1)}, bf16[2,2,10,16,128]{4,3,2,1,0:T(8,128)(2,1)S(1)}, u32[]{:S(2)}, u32[]{:S(2)}) collective-permute-start(bf16[2,2,10,16,128]{4,3,2,1,0:T(8,128)(2,1)S(1)} %bitcast.140), channel_id=1, source_target_pairs={{0,12},{1,5},{2,14},{3,7},{4,8},{5,1},{6,10},{7,3},{8,4},{9,13},{1... | collective-permute-start | bytes 491528 | tf_op jit(solution)/shard_map/ppermute | solution.py:713
  340.6 6.8 %collective-permute-start.33 = (bf16[2,2,11,16,128]{4,3,2,1,0:T(8,128)(2,1)S(1)}, bf16[2,2,11,16,128]{4,3,2,1,0:T(8,128)(2,1)S(1)}, u32[]{:S(2)}, u32[]{:S(2)}) collective-permute-start(bf16[2,2,11,16,128]{4,3,2,1,0:T(8,128)(2,1)S(1)} %bitcast.139), channel_id=1, source_target_pairs={{0,12},{1,5},{2,14},{3,7},{4,8},{5,1},{6,10},{7,3},{8,4},{9,13},{1... | collective-permute-start | bytes 540680 | tf_op jit(solution)/shard_map/ppermute | solution.py:713
  349.8 10.8 %collective-permute-start.34 = (bf16[2,53,16,128]{3,2,1,0:T(8,128)(2,1)}, bf16[2,53,16,128]{3,2,1,0:T(8,128)(2,1)S(1)}, u32[]{:S(2)}, u32[]{:S(2)}) collective-permute-start(bf16[2,53,16,128]{3,2,1,0:T(8,128)(2,1)} %get-tuple-element.210), channel_id=1, source_target_pairs={{0,2},{1,19},{2,0},{3,17},{4,6},{5,23},{6,4},{7,21},{8,10},{9,27},... | collective-permute-start | bytes 1302536 | tf_op jit(solution)/shard_map/ppermute | solution.py:713
  360.7 7.2 %collective-permute-start.35 = (bf16[53,16,128]{2,1,0:T(8,128)(2,1)S(1)}, bf16[53,16,128]{2,1,0:T(8,128)(2,1)S(1)}, u32[]{:S(2)}, u32[]{:S(2)}) collective-permute-start(bf16[53,16,128]{2,1,0:T(8,128)(2,1)S(1)} %get-tuple-element.212), channel_id=1, source_target_pairs={{0,18},{1,3},{2,16},{3,1},{4,22},{5,7},{6,20},{7,5},{8,26},{9,11},... | collective-permute-start | bytes 651272 | tf_op jit(solution)/shard_map/ppermute | solution.py:713
  369.1 3.2 collective-permute-start.36
  (21 other events, 37.5 us)
